TPU v7x, 512 devices: a whole 4x8x8 slice. The times are simulated.
512 devices in a mesh: frame: 64 (over y, z), band: 8 (over x, core).
Axes of the slice: x: 4, y: 8, z: 8, core: 2. Of those that a mesh axis runs over, the one named last changes fastest.
Arguments:
- tokens: bfloat16 [8192, 3072], P(('frame', 'band')), may hold values from -6 to 6
- qkv_weight: bfloat16 [3072, 3, 2048], P('frame', None, 'band'), may hold values from -1 to 1, as said below
- out_weight: bfloat16 [2048, 3072], P('frame', 'band'), may hold values from -0.125 to 0.125
- head_kind: int32 [16], P('band'), may hold values from 0 to 1
Outputs:
- attended: bfloat16 [8192, 3072], P(('frame', 'band'))
Inputs may be any that keep to these rules, and one draw needn't show every extreme that they name: `head_kind`: 0 marks a spatial head, 1 a temporal head. `qkv_weight`: entries lie within 4 * 3072^-0.5 in magnitude.
All inputs are finite; a program needn't handle non-finite values.
Results may differ from a plain program's by a relative error of at most 0.022.
Values may be sent and summed in bfloat16 or wider, within the bound.
A program may use at most 64 MiB of HBM per device.

v0:
```python
import jax
import jax.numpy as jnp
from jax import lax
from jax.sharding import PartitionSpec as P


def softmax_rows(scores):
    largest = jnp.max(scores, axis=-1, keepdims=True)
    raised = jnp.exp(scores - largest)
    return (raised / jnp.sum(raised, axis=-1, keepdims=True)).astype(jnp.bfloat16)


def spatial_heads(queries, keys_all, values_all, factor):
    scores = (
        jnp.einsum("phe,qhe->hpq", queries, keys_all, preferred_element_type=jnp.float32) * factor
    )
    weights = softmax_rows(scores)
    return jnp.einsum(
        "hpq,qhe->phe", weights, values_all, preferred_element_type=jnp.float32
    ).astype(jnp.bfloat16)


def body(tokens, qkv_weight, out_weight, head_kind):
    frame_count = lax.axis_size("frame")
    frame_rows = lax.all_gather(tokens, "band", axis=0, tiled=True)
    positions = frame_rows.shape[0]
    per_head = qkv_weight.shape[2]
    columns = 3 * per_head
    heads_here = head_kind.shape[0]
    head_size = per_head // heads_here
    scale_factor = head_size ** (-0.5)
    full_weight = lax.all_gather(qkv_weight, "frame", axis=0, tiled=True)
    summed = jnp.dot(
        frame_rows,
        full_weight.reshape(full_weight.shape[0], columns),
        preferred_element_type=jnp.float32,
    )
    rounded = summed.astype(jnp.bfloat16)
    projected = rounded.reshape(positions, 3, heads_here, head_size)
    queries = projected[:, 0]
    keys_all = projected[:, 1]
    values_all = projected[:, 2]
    spatial = spatial_heads(queries, keys_all, values_all, scale_factor)
    group_size = positions // frame_count
    packed = rounded.reshape(1, frame_count, group_size, columns)
    received = lax.all_to_all(packed, "frame", split_axis=1, concat_axis=0, tiled=True)
    unpacked = received.reshape(received.shape[0], received.shape[2], 3, heads_here, head_size)
    time_queries = unpacked[:, :, 0]
    time_keys = unpacked[:, :, 1]
    time_values = unpacked[:, :, 2]
    scores = (
        jnp.einsum("fghe,kghe->ghfk", time_queries, time_keys, preferred_element_type=jnp.float32)
        * scale_factor
    )
    weights = softmax_rows(scores)
    mixed = jnp.einsum(
        "ghfk,kghe->fghe", weights, time_values, preferred_element_type=jnp.float32
    ).astype(jnp.bfloat16)
    outgoing = mixed.reshape(received.shape[0], 1, received.shape[2], per_head)
    temporal = lax.all_to_all(outgoing, "frame", split_axis=0, concat_axis=1, tiled=True)
    temporal = temporal.reshape(positions, heads_here, head_size)
    chosen = jnp.where((head_kind == 1)[None, :, None], temporal, spatial).reshape(
        positions, per_head
    )
    weight_rows = lax.all_gather(out_weight, "frame", axis=0, tiled=True)
    own_weight = lax.all_to_all(weight_rows, "band", split_axis=0, concat_axis=1, tiled=True)
    return lax.psum_scatter(
        jnp.dot(chosen, own_weight, preferred_element_type=jnp.float32).astype(jnp.bfloat16),
        "band",
        scatter_dimension=0,
        tiled=True,
    )


def solution(mesh):
    return jax.shard_map(
        body,
        mesh=mesh,
        in_specs=(
            P(("frame", "band"), None),
            P("frame", None, "band"),
            P("frame", "band"),
            P("band"),
        ),
        out_specs=P(("frame", "band"), None),
        check_vma=False,
    )
```

profile of v0, /device:TPU:1, one launch (start us, length us, event | category | flops | bytes accessed | tf_op | source)
XLA Modules:
  0.0 273.4 jit_solution(14256164618781392550)
XLA Ops:
  6.5 0.7 all-gather.5.cloned.1.call-update
  7.3 0.7 all-gather.3.cloned.1.call-update
  8.0 86.7 %all-gather.5.cloned.1.call-done = bf16[2048,384]{1,0:T(8,128)(2,1)} async-done(((bf16[32,384]{1,0:T(8,128)(2,1)}), bf16[2048,384]{1,0:T(8,128)(2,1)}) %all-gather.5.cloned.1.call-update) | async-done | bytes 1572880 | tf_op jit(solution)/shard_map/all_gather | solution.py:65
  94.7 9.1 %all-to-all-start.2 = ((bf16[8,256,384]{2,1,0:T(8,128)(2,1)}), bf16[8,256,384]{2,1,0:T(8,128)(2,1)S(1)}, u32[]{:S(2)}, u32[]{:S(2)}) async-start(bf16[8,256,384]{2,1,0:T(8,128)(2,1)} %bitcast.57), calls=%async_computation.2 | async-start | bytes 3145728 | tf_op jit(solution)/shard_map/all_to_all | solution.py:66
  103.8 29.8 %all_gather.9 = bf16[128,3072]{1,0:T(8,128)(2,1)S(1)} all-gather(bf16[16,3072]{1,0:T(8,128)(2,1)S(1)} %copy-done), channel_id=1, replica_groups=mesh['frame'=64,'band'=8] {'band'}, dimensions={0}, use_global_device_ids=true | all-gather | bytes 884736 | tf_op jit(solution)/shard_map/all_gather | solution.py:25
  133.5 49.9 %all-gather.3.cloned.1.call-done = bf16[3072,3,256]{2,0,1:T(8,128)(2,1)} async-done(((bf16[48,3,256]{2,0,1:T(8,128)(2,1)}), bf16[3072,3,256]{2,0,1:T(8,128)(2,1)}) %all-gather.3.cloned.1.call-update) | async-done | bytes 4718608 | tf_op jit(solution)/shard_map/all_gather | solution.py:32
  183.4 6.7 %copy.37 = bf16[3072,3,256]{0,2,1:T(8,128)(2,1)} copy(bf16[3072,3,256]{2,0,1:T(8,128)(2,1)} %all-gather.3.cloned.1.call-done) | data formatting | bytes 9437184 | tf_op jit(solution)/shard_map/all_gather | solution.py:32
  190.1 4.0 %convolution_convert_fusion.1 = bf16[128,768]{1,0:T(8,128)(2,1)S(1)} fusion(bf16[128,3072]{1,0:T(8,128)(2,1)S(1)} %all_gather.9, bf16[3072,768]{0,1:T(8,128)(2,1)} %bitcast.54), kind=kOutput, calls=%fused_computation.3 | convolution fusion | flops 604078080 | bytes 5701632 | tf_op jit(solution)/shard_map/dot_general | solution.py:33
  194.2 0.7 reshape.38
  194.9 8.3 %all-to-all-start = ((bf16[1,64,2,768]{3,2,0,1:T(2,128)(2,1)}), bf16[1,64,2,768]{3,2,0,1:T(2,128)(2,1)S(1)}, u32[]{:S(2)}, u32[]{:S(2)}) async-start(bf16[1,64,2,768]{3,2,0,1:T(2,128)(2,1)} %bitcast.1), calls=%async_computation | async-start | bytes 393216 | tf_op jit(solution)/shard_map/all_to_all | solution.py:46
  203.2 0.8 copy.51
  204.0 0.1 fusion.16
  204.2 10.9 %all-to-all-done = bf16[1,64,2,768]{3,2,0,1:T(2,128)(2,1)S(1)} async-done(((bf16[1,64,2,768]{3,2,0,1:T(2,128)(2,1)}), bf16[1,64,2,768]{3,2,0,1:T(2,128)(2,1)S(1)}, u32[]{:S(2)}, u32[]{:S(2)}) %all-to-all-start) | async-done | bytes 196640 | tf_op jit(solution)/shard_map/all_to_all | solution.py:46
  215.4 0.2 fusion.18
  215.6 0.1 convolution_multiply_fusion.1
  215.7 0.2 fusion.6
  216.1 0.7 reshape.45
  216.7 4.6 %all-to-all-start.1 = ((bf16[64,1,2,256]{3,2,1,0:T(2,128)(2,1)}), bf16[64,1,2,256]{3,2,1,0:T(2,128)(2,1)S(1)}, u32[]{:S(2)}, u32[]{:S(2)}) async-start(bf16[64,1,2,256]{3,2,1,0:T(2,128)(2,1)} %reshape.45), calls=%async_computation.1 | async-start | bytes 131072 | tf_op jit(solution)/shard_map/all_to_all | solution.py:60
  221.4 0.2 convolution_multiply_fusion
  221.7 0.2 fusion.19
  221.9 10.5 %all-to-all-done.1 = bf16[64,1,2,256]{3,2,1,0:T(2,128)(2,1)S(1)} async-done(((bf16[64,1,2,256]{3,2,1,0:T(2,128)(2,1)}), bf16[64,1,2,256]{3,2,1,0:T(2,128)(2,1)S(1)}, u32[]{:S(2)}, u32[]{:S(2)}) %all-to-all-start.1) | async-done | bytes 65568 | tf_op jit(solution)/shard_map/all_to_all | solution.py:60
  232.6 0.2 fusion.8
  232.8 1.5 convolution_convert_fusion
  234.4 32.5 %reduce-scatter.2.cloned.1.call-done = bf16[16,3072]{1,0:T(8,128)(2,1)} async-done(((bf16[128,3072]{1,0:T(8,128)(2,1)}), bf16[16,3072]{1,0:T(8,128)(2,1)}) %reduce-scatter.2.cloned.1.call-update) | async-done | bytes 98320 | tf_op jit(solution)/shard_map/reduce_scatter | solution.py:67
  (17 shorter events, 0.8 us)
Async XLA Ops:
  6.5 88.2 %all-gather.5.cloned.1.call-start = ((), (), s32[]{:S(2)}) async-start(), calls=%async_computation.5 | async-start | bytes 1597440 | tf_op jit(solution)/shard_map/all_gather | solution.py:65
  7.3 176.2 %all-gather.3.cloned.1.call-start = ((), (), s32[]{:S(2)}) async-start(), calls=%async_computation.4 | async-start | bytes 4792320 | tf_op jit(solution)/shard_map/all_gather | solution.py:32
  94.7 9.1 %copy-start = (bf16[16,3072]{1,0:T(8,128)(2,1)S(1)}, bf16[16,3072]{1,0:T(8,128)(2,1)}, u32[]{:S(2)}) copy-start(bf16[16,3072]{1,0:T(8,128)(2,1)} %param.4) | copy-start | bytes 294916
  94.7 100.2 %all-to-all-start.2 = ((bf16[8,256,384]{2,1,0:T(8,128)(2,1)}), bf16[8,256,384]{2,1,0:T(8,128)(2,1)S(1)}, u32[]{:S(2)}, u32[]{:S(2)}) async-start(bf16[8,256,384]{2,1,0:T(8,128)(2,1)} %bitcast.57), calls=%async_computation.2 | async-start | bytes 3145728 | tf_op jit(solution)/shard_map/all_to_all | solution.py:66
  190.1 13.1 %copy-start.1 = (s32[2]{0:T(128)S(1)}, s32[2]{0:T(128)}, u32[]{:S(2)}) copy-start(s32[2]{0:T(128)} %param.7) | copy-start | bytes 28
  194.9 20.2 %all-to-all-start = ((bf16[1,64,2,768]{3,2,0,1:T(2,128)(2,1)}), bf16[1,64,2,768]{3,2,0,1:T(2,128)(2,1)S(1)}, u32[]{:S(2)}, u32[]{:S(2)}) async-start(bf16[1,64,2,768]{3,2,0,1:T(2,128)(2,1)} %bitcast.1), calls=%async_computation | async-start | bytes 393216 | tf_op jit(solution)/shard_map/all_to_all | solution.py:46
  216.7 15.7 %all-to-all-start.1 = ((bf16[64,1,2,256]{3,2,1,0:T(2,128)(2,1)}), bf16[64,1,2,256]{3,2,1,0:T(2,128)(2,1)S(1)}, u32[]{:S(2)}, u32[]{:S(2)}) async-start(bf16[64,1,2,256]{3,2,1,0:T(2,128)(2,1)} %reshape.45), calls=%async_computation.1 | async-start | bytes 131072 | tf_op jit(solution)/shard_map/all_to_all | solution.py:60
  221.4 45.5 %reduce-scatter.2.cloned.1.call-start = ((), (), s32[]{:S(2)}) async-start(), calls=%async_computation.6 | async-start | bytes 884736 | tf_op jit(solution)/shard_map/reduce_scatter | solution.py:67
Sparse Core Ops, SparseCore 0:
  10.4 84.2 all-gather.4
  97.7 85.6 all-gather.2
  234.5 32.3 reduce-scatter.1
where the time goes:
time: 275 us; the launch traced here: 273 us
  waiting for transfers between devices  192 us (70%)
  blocking collectives  29.8 us (11%)
  starting transfers between devices  22 us (8%)
  between operations  13.2 us (5%)
  local copies, waits for them, and re-layouts  9.71 us (4%)
  matrix products  6.73 us (2%)
    all_gather x1, waiting for transfers between devices, body(): weight_rows = lax.all_gather(out_weight, 'frame', axis=0, tiled=True)  86.7 us
    all_gather x1, waiting for transfers between devices, body(): full_weight = lax.all_gather(qkv_weight, 'frame', axis=0, tiled=True)  49.9 us
    reduce_scatter x1, waiting for transfers between devices, body(): lax.psum_scatter(jnp.dot(chosen, own_weight, preferred_element_type=jnp.f...  32.5 us
    all_gather x1, blocking collectives, body(): frame_rows = lax.all_gather(tokens, 'band', axis=0, tiled=True)  29.8 us
    all_to_all x1, waiting for transfers between devices, body(): lax.all_to_all(packed, 'frame', split_axis=1, concat_axis=0, tiled=True)  10.9 us
    all_to_all x1, waiting for transfers between devices, body(): lax.all_to_all(outgoing, 'frame', split_axis=0, concat_axis=1, tiled=True)  10.5 us
    all_to_all x1, starting transfers between devices, body(): lax.all_to_all(weight_rows, 'band', split_axis=0, concat_axis=1, tiled=True)  9.08 us
    all_to_all x1, starting transfers between devices, body(): lax.all_to_all(packed, 'frame', split_axis=1, concat_axis=0, tiled=True)  8.26 us
  transfers between devices with their start and end apart: 6, of which 5 were waited for; matrix products, arithmetic and copies ran while one was open for 5% of the time, Pallas kernels for 0%

commit v1 on v0

v1 whole, which is shorter than its diff:
```python
import jax
import jax.numpy as jnp
from jax import lax
from jax.experimental import pallas as pl
from jax.experimental.pallas import tpu as pltpu
from jax.sharding import PartitionSpec as P

MESH = pl.DeviceIdType.MESH
NX = 4
NY = 8
NZ = 8
PAIRS = NZ // 2
BANDS = 2 * NX
PEERS = NY * PAIRS
HEAD = 128
POSITIONS = 128
ROWS = 2 * POSITIONS
SHARE = POSITIONS // PEERS
DEPTH = 48
WIDTH = 384


def remote(src, dst, send_sem, recv_sem, device):
    return pltpu.make_async_remote_copy(
        src_ref=src,
        dst_ref=dst,
        send_sem=send_sem,
        recv_sem=recv_sem,
        device_id=device,
        device_id_type=MESH,
    )


def await_bytes(ref, sem):
    pltpu.make_async_copy(ref, ref, sem).wait()


def attend(queries, keys, values, bias):
    scores = lax.dot_general(
        queries, keys, (((1,), (1,)), ((), ())), preferred_element_type=jnp.float32
    ) * (HEAD**-0.5)
    if bias is not None:
        scores = scores + bias
    raised = jnp.exp(scores - jnp.max(scores, axis=-1, keepdims=True))
    probs = (raised / jnp.sum(raised, axis=-1, keepdims=True)).astype(jnp.bfloat16)
    return jnp.dot(probs, values, preferred_element_type=jnp.float32)


def wrap(value, size):
    return lax.rem(value + 8 * size, size)


def hops(size):
    return (size // 2, (size - 1) // 2)


def wander(place):
    if isinstance(place, int):
        return (place + 1) // 2 * (2 * (place % 2) - 1)
    return lax.div(place + 1, 2) * (2 * lax.rem(place, 2) - 1)


class Grid:
    def __init__(self, block, device, here, sizes, sign, sems):
        self.block = block
        self.device = device
        self.first, self.second = here
        self.n_first, self.n_second = sizes
        self.sign = sign
        self.send, self.recv1, self.recv2 = sems

    def turn(self, way):
        return self.sign if way == 0 else -self.sign

    def to_second(self, block, way, step, place):
        there = wrap(self.second + self.turn(way), self.n_second)
        remote(
            block,
            block,
            self.send.at[1, way],
            self.recv2.at[way, step, place],
            self.device(self.first, there),
        ).start()

    def begin(self, part):
        own = part(self.first, self.second)
        for way in range(2):
            if hops(self.n_second)[way]:
                self.to_second(own, way, 0, 0)

        for place in range(1, self.n_first // 2 + 1):
            self.to_first(own, place, self.sign * wander(place))

    def to_first(self, block, place, by):
        there = wrap(self.first + by, self.n_first)
        remote(
            block,
            block,
            self.send.at[0, 0],
            self.recv1.at[place],
            self.device(there, self.second),
        ).start()

    def along_first(self, place):
        block = self.block(
            wrap(self.first - self.sign * wander(place), self.n_first), self.second
        )
        await_bytes(block, self.recv1.at[place])
        half = self.n_first // 4
        if isinstance(place, int) and place == 2 * half - 1:
            self.to_first(block, self.n_first - 1, self.sign * half)
            if half > 1:
                self.to_first(block, self.n_first - 3, self.sign)
        if isinstance(place, int) and place == 2 * half and half > 1:
            self.to_first(block, self.n_first - 2, -self.sign)
        for way in range(2):
            if hops(self.n_second)[way]:
                self.to_second(block, way, 0, place)

    def along_second(self, step, place):
        for way in range(2):
            count = hops(self.n_second)[way]
            if step > count:
                continue
            block = self.block(
                wrap(self.first - self.sign * wander(place), self.n_first),
                wrap(self.second - self.turn(way) * step, self.n_second),
            )
            await_bytes(block, self.recv2.at[way, step - 1, place])
            if step < count:
                self.to_second(block, way, step, place)


def kernel(
    tokens,
    qkv,
    out_weight,
    kind_hbm,
    out,
    wbuf,
    obuf,
    tbuf,
    msg,
    fin,
    rmsg,
    rfin,
    cbuf,
    mbuf,
    sbuf,
    qkv_sum,
    total,
    by_peer,
    by_frame,
    bias,
    kind,
    own_sem,
    z_send,
    z_recv,
    w_send,
    w_recv1,
    w_recv2,
    o_send,
    o_recv1,
    o_recv2,
    t_send,
    t_recv,
    s_send,
    s_recv,
    a_send,
    a_recv,
    m_send,
    m_recv,
    n_send,
    n_recv,
    f_send,
    f_recv,
):
    frame = lax.axis_index("frame")
    band = lax.axis_index("band")
    y, z = lax.div(frame, NZ), lax.rem(frame, NZ)
    x, core = lax.div(band, 2), lax.rem(band, 2)
    across = z + (y - z) * core
    along = y + (z - y) * core
    pair, odd = lax.div(across, 2), lax.rem(across, 2)
    other = 1 - odd
    sign = 1 - 2 * core
    sibling_band = 2 * x + 1 - core
    sibling = (frame, sibling_band)
    sibling_odd = lax.rem(y + (z - y) * core, 2)
    me = along * PAIRS + pair

    def frame_at(along_there, across_there):
        return along_there * (NZ - (NZ - 1) * core) + across_there * (1 + (NZ - 1) * core)

    beside = frame_at(along, 2 * pair + other)

    def band_at(step):
        return 2 * wrap(x + step, NX) + core

    def peer(index):
        return (frame_at(lax.div(index, PAIRS), 2 * lax.rem(index, PAIRS) + odd), band)

    barrier = pltpu.get_barrier_semaphore()

    def greet(device):
        pl.semaphore_signal(barrier, inc=1, device_id=device, device_id_type=MESH)

    greet(sibling)
    greet((beside, sibling_band))
    for step in (1, -1):
        greet((y * NZ + wrap(z + step, NZ), band))
        greet((wrap(y + step, NY) * NZ + z, band))
        greet((frame_at(along, 2 * wrap(pair + step, PAIRS) + odd), band))
    for step in range(1, NX):
        greet((frame, band_at(step)))

    def head_columns(which):
        return qkv.at[:, :, pl.ds(pl.multiple_of(which * HEAD, HEAD), HEAD)]

    own = [
        pltpu.make_async_copy(head_columns(odd), wbuf.at[:, along, pair, odd], own_sem.at[0]),
        pltpu.make_async_copy(out_weight.at[0:16], obuf.at[0, y, z], own_sem.at[1]),
        pltpu.make_async_copy(out_weight.at[16:32], obuf.at[1, z, y], own_sem.at[2]),
        pltpu.make_async_copy(tokens, tbuf.at[odd, band], own_sem.at[3]),
        pltpu.make_async_copy(kind_hbm, kind, own_sem.at[4]),
    ]
    for copy in own:
        copy.start()
    pl.semaphore_wait(barrier, 8 + NX - 1)

    remote(
        head_columns(other), wbuf.at[:, along, pair, odd], z_send.at[0], z_recv.at[0], (beside, band)
    ).start()
    beside_z = y * NZ + z + 1 - 2 * lax.rem(z, 2)
    beside_y = (y + 1 - 2 * lax.rem(y, 2)) * NZ + z
    remote(
        tokens, tbuf.at[lax.rem(z, 2), band], z_send.at[1], z_recv.at[1 + core], (beside_z, 2 * x)
    ).start()
    remote(
        tokens, tbuf.at[lax.rem(y, 2), band], z_send.at[2], z_recv.at[1 + core], (beside_y, 2 * x + 1)
    ).start()

    grid = Grid(
        lambda first, second: wbuf.at[:, second, first],
        lambda first, second: (frame_at(second, 2 * first + odd), band),
        (pair, along),
        (PAIRS, NY),
        sign,
        (w_send, w_recv1, w_recv2),
    )

    def begin(which):
        grid.begin(lambda first, second: wbuf.at[:, second, first, which])

    def token_along_x(which, block):
        for step in (1, NX - 1, 2):
            remote(
                block, block, t_send.at[which, step], t_recv.at[which, step], (frame, band_at(step))
            ).start()

    for copy in own:
        copy.wait()
    begin(odd)
    token_along_x(0, tbuf.at[odd, band])
    remote(
        tbuf.at[odd, band], tbuf.at[sibling_odd, band], s_send.at[0], s_recv.at[0], sibling
    ).start()

    tall = lax.broadcasted_iota(jnp.int32, (ROWS, ROWS), 0)
    wide = lax.broadcasted_iota(jnp.int32, (ROWS, ROWS), 1)

    def origin(row):
        return (
            lax.rem(lax.div(row, SHARE), 2) * POSITIONS
            + lax.div(row, 2 * SHARE) * SHARE
            + lax.rem(row, SHARE)
        )

    qkv_sum[...] = jnp.zeros_like(qkv_sum)
    by_peer[...] = jnp.where(wide == origin(tall), 1.0, 0.0).astype(jnp.bfloat16)
    by_frame[...] = jnp.where(tall == origin(wide), 1.0, 0.0).astype(jnp.bfloat16)
    bias[...] = jnp.where(lax.rem(tall, SHARE) == lax.rem(wide, SHARE), 0.0, -1e30)

    await_bytes(wbuf.at[:, along, pair, other], z_recv.at[0])
    begin(other)
    for which in range(2):
        await_bytes(tbuf.at[other, 2 * x + which], z_recv.at[1 + which])
        token_along_x(1 + which, tbuf.at[other, 2 * x + which])

    def out_block(half, first, second):
        return obuf.at[half, second, first]

    def out_here(half):
        return (z, y) if half == 0 else (y, z)

    def out_device(half, first, second):
        return (second * NZ + first if half == 0 else first * NZ + second, band)

    def turn(way):
        return sign if way == 0 else -sign

    def out_send1(half, way, step, block):
        first, second = out_here(half)
        there = wrap(first + turn(way), NY)
        remote(
            block,
            block,
            o_send.at[half, 0, way],
            o_recv1.at[half, way, step],
            out_device(half, there, second),
        ).start()

    def out_send2(half, way, step, chunk):
        first, second = out_here(half)
        there = wrap(second + turn(way), NY)
        remote(
            chunk,
            chunk,
            o_send.at[half, 1, way],
            o_recv2.at[half, way, step],
            out_device(half, first, there),
        ).start()

    def out_along_first(step):
        for half in range(2):
            first, second = out_here(half)
            for way in range(2):
                if step > hops(NY)[way]:
                    continue
                block = obuf.at[half, second, wrap(first - turn(way) * step, NY)]
                if step:
                    await_bytes(block, o_recv1.at[half, way, step - 1])
                if step < hops(NY)[way]:
                    out_send1(half, way, step, block)

    def out_along_second(step):
        for half in range(2):
            first, second = out_here(half)
            for way in range(2):
                if step > hops(NY)[way]:
                    continue
                chunk = obuf.at[half, wrap(second - turn(way) * step, NY)]
                if step:
                    await_bytes(chunk, o_recv2.at[half, way, step - 1])
                if step < hops(NY)[way]:
                    out_send2(half, way, step, chunk)

    out_along_first(0)
    for place in range(1, PAIRS):
        grid.along_first(place)

    def ring_step(step):
        def one(place, carry):
            grid.along_second(step, place)
            return carry

        lax.fori_loop(0, PAIRS, one, 0)

    ring_step(1)
    out_along_first(1)
    for hop in (1, NX - 1, 2):
        from_band = band_at(-hop)
        await_bytes(tbuf.at[odd, from_band], t_recv.at[0, hop])
        remote(
            tbuf.at[odd, from_band],
            tbuf.at[sibling_odd, from_band],
            s_send.at[hop],
            s_recv.at[hop],
            sibling,
        ).start()
    ring_step(2)
    out_along_first(2)
    ring_step(3)
    out_along_first(3)
    out_along_first(4)
    out_along_second(0)
    for hop in range(NX):
        from_band = 2 * wrap(x - hop, NX) + 1 - core
        await_bytes(tbuf.at[odd, from_band], s_recv.at[hop])
        if hop:
            for which in range(2):
                await_bytes(
                    tbuf.at[other, 2 * wrap(x - hop, NX) + which], t_recv.at[1 + which, hop]
                )
    ring_step(4)

    chunk = 2 * NZ * DEPTH

    def project(step, right):
        at = pl.ds(pl.multiple_of(step * chunk, HEAD), chunk)
        qkv_sum[...] += jnp.dot(
            tbuf[:, :, :, at].reshape(ROWS, chunk),
            jnp.concatenate([right(slot) for slot in range(3)], axis=1),
            preferred_element_type=jnp.float32,
        )

    @pl.when(core == 0)
    def _():
        def one(step, carry):
            project(step, lambda slot: wbuf[slot, pl.ds(2 * step, 2)].reshape(chunk, HEAD))
            return carry

        lax.fori_loop(0, NY // 2, one, 0)

    @pl.when(core == 1)
    def _():
        def one(step, carry):
            project(
                step,
                lambda slot: jnp.concatenate(
                    [
                        wbuf[slot, :, step, parity].reshape(chunk // 2, HEAD)
                        for parity in range(2)
                    ],
                    axis=0,
                ),
            )
            return carry

        lax.fori_loop(0, NY // 2, one, 0)

    rounded = qkv_sum[...].astype(jnp.bfloat16)

    msg[...] = (
        jnp.dot(by_peer[...], rounded, preferred_element_type=jnp.float32)
        .reshape(msg.shape)
        .astype(jnp.bfloat16)
    )

    def exchange(stage, source, target):
        def send(step, carry):
            there = lax.rem(me + step, PEERS)
            remote(
                source.at[there], target.at[me], a_send.at[stage], a_recv.at[stage], peer(there)
            ).start()
            return carry

        pltpu.make_async_copy(source.at[me], target.at[me], a_recv.at[stage]).start()
        lax.fori_loop(1, PEERS, send, 0)

    exchange(0, msg, fin)
    out_along_second(1)
    spatial = jnp.concatenate(
        [
            attend(
                rounded[at : at + POSITIONS, :HEAD],
                rounded[at : at + POSITIONS, HEAD : 2 * HEAD],
                rounded[at : at + POSITIONS, 2 * HEAD :],
                None,
            )
            for at in (0, POSITIONS)
        ],
        axis=0,
    ).astype(jnp.bfloat16)
    await_bytes(wbuf.at[:, 0, 0, 0], z_send.at[0])
    await_bytes(tbuf.at[0, 0], z_send.at[1])
    await_bytes(tbuf.at[0, 0], z_send.at[2])
    await_bytes(wbuf.at[:, 0, 0 : PAIRS - 1], w_send.at[0, 0])
    for way in range(2):
        await_bytes(wbuf.at[:, 0 : hops(NY)[way]], w_send.at[1, way])
        for half in range(2):
            await_bytes(obuf.at[half, 0, 0 : hops(NY)[way]], o_send.at[half, 0, way])
    for hop in range(NX):
        await_bytes(tbuf.at[0, 0], s_send.at[hop])
        if hop:
            for which in range(3):
                await_bytes(tbuf.at[0, 0], t_send.at[which, hop])
    await_bytes(fin, a_recv.at[0])
    out_along_second(2)
    laid = fin[...].reshape(ROWS, 3 * HEAD)
    mixed = attend(laid[:, :HEAD], laid[:, HEAD : 2 * HEAD], laid[:, 2 * HEAD :], bias[...])
    rmsg[...] = mixed.reshape(rmsg.shape).astype(jnp.bfloat16)
    exchange(1, rmsg, rfin)
    await_bytes(msg.at[0 : PEERS - 1], a_send.at[0])
    await_bytes(rfin, a_recv.at[1])
    out_along_second(3)
    back = jnp.dot(
        by_frame[...], rfin[...].reshape(ROWS, HEAD), preferred_element_type=jnp.float32
    ).astype(jnp.bfloat16)
    temporal = jnp.full((ROWS, HEAD), kind[odd], jnp.int32) == 1
    cbuf[...] = jnp.where(temporal, back, spatial).reshape(cbuf.shape)

    for step in (1, NX - 1, 2):
        remote(
            cbuf.at[odd],
            mbuf.at[band, odd],
            m_send.at[0, step],
            m_recv.at[0, step],
            (frame, band_at(step)),
        ).start()
    for step in (1, NX - 1, 2, 0):
        remote(
            cbuf.at[other],
            mbuf.at[band, odd],
            m_send.at[1, step],
            m_recv.at[1, step],
            (beside, band_at(step)),
        ).start()
    remote(
        cbuf.at[odd], mbuf.at[band, odd], n_send.at[0, 0], n_recv.at[0, 0], sibling
    ).start()
    last = pltpu.make_async_copy(cbuf.at[odd], mbuf.at[band, odd], m_recv.at[0, 0])
    last.start()
    for which, hop in ((1, 0), (0, 1), (0, 3), (1, 1), (1, 3), (0, 2), (1, 2)):
        block = mbuf.at[band_at(-hop), odd if which == 0 else other]
        await_bytes(block, m_recv.at[which, hop])
        remote(block, block, n_send.at[which, hop], n_recv.at[which, hop], sibling).start()
    out_along_second(4)
    last.wait()

    def project_out(source):
        left = jnp.concatenate([mbuf[source, 0], mbuf[source, 1]], axis=1)
        right = jnp.stack([obuf[0, source], obuf[1, :, source]], axis=1).reshape(
            2 * HEAD, WIDTH
        )
        return jnp.dot(left, right, preferred_element_type=jnp.float32)

    def own_core(hop, carry):
        total[...] += project_out(band_at(-hop))
        return carry

    def other_core(hop, carry):
        source = 2 * wrap(x - hop, NX) + 1 - core
        for which in range(2):
            await_bytes(
                mbuf.at[source, sibling_odd if which == 0 else 1 - sibling_odd],
                n_recv.at[which, hop],
            )
        total[...] += project_out(source)
        return carry

    total[...] = jnp.zeros_like(total)
    lax.fori_loop(0, NX, own_core, 0)
    lax.fori_loop(0, NX, other_core, 0)
    sbuf[...] = total[...].astype(jnp.bfloat16).reshape(sbuf.shape)

    def columns(which):
        return out.at[:, pl.ds(pl.multiple_of(which * WIDTH, HEAD), WIDTH)]

    for step in range(1, BANDS):
        there = wrap(band + step, BANDS)
        remote(
            sbuf.at[there], columns(band), f_send.at[step], f_recv.at[step], (frame, there)
        ).start()
    last = pltpu.make_async_copy(sbuf.at[band], columns(band), f_send.at[0])
    last.start()
    for step in range(1, BANDS):
        await_bytes(columns(wrap(band - step, BANDS)), f_recv.at[step])
    last.wait()

    await_bytes(rmsg.at[0 : PEERS - 1], a_send.at[1])
    for which in range(2):
        for hop in range(NX):
            if hop or which:
                await_bytes(cbuf.at[0], m_send.at[which, hop])
            await_bytes(cbuf.at[0], n_send.at[which, hop])
    for half in range(2):
        for way in range(2):
            await_bytes(obuf.at[half, 0 : hops(NY)[way]], o_send.at[half, 1, way])
    for step in range(1, BANDS):
        await_bytes(sbuf.at[0], f_send.at[step])


def body(tokens, qkv_weight, out_weight, head_kind):
    bf16 = jnp.bfloat16
    dma = pltpu.SemaphoreType.DMA
    hbm = pl.BlockSpec(memory_space=pltpu.HBM)
    return pl.pallas_call(
        kernel,
        out_shape=jax.ShapeDtypeStruct(tokens.shape, tokens.dtype),
        in_specs=[hbm] * 4,
        out_specs=hbm,
        scratch_shapes=[
            pltpu.VMEM((3, NY, PAIRS, 2, DEPTH, HEAD), bf16),
            pltpu.VMEM((2, 8, 8, 16, WIDTH), bf16),
            pltpu.VMEM((2, BANDS) + tokens.shape, bf16),
            pltpu.VMEM((PEERS, 2 * SHARE, 3 * HEAD), bf16),
            pltpu.VMEM((PEERS, 2 * SHARE, 3 * HEAD), bf16),
            pltpu.VMEM((PEERS, 2 * SHARE, HEAD), bf16),
            pltpu.VMEM((PEERS, 2 * SHARE, HEAD), bf16),
            pltpu.VMEM((2, POSITIONS, HEAD), bf16),
            pltpu.VMEM((BANDS, 2, POSITIONS, HEAD), bf16),
            pltpu.VMEM((BANDS, 16, WIDTH), bf16),
            pltpu.VMEM((ROWS, 3 * HEAD), jnp.float32),
            pltpu.VMEM((POSITIONS, WIDTH), jnp.float32),
            pltpu.VMEM((ROWS, ROWS), bf16),
            pltpu.VMEM((ROWS, ROWS), bf16),
            pltpu.VMEM((ROWS, ROWS), jnp.float32),
            pltpu.SMEM((2,), jnp.int32),
            dma((5,)),
            dma((3,)),
            dma((3,)),
            dma((2, 2)),
            dma((4,)),
            dma((2, 4, 4)),
            dma((2, 2, 2)),
            dma((2, 2, 4)),
            dma((2, 2, 4)),
            dma((3, NX)),
            dma((3, NX)),
            dma((NX,)),
            dma((NX,)),
            dma((2,)),
            dma((2,)),
            dma((2, NX)),
            dma((2, NX)),
            dma((2, NX)),
            dma((2, NX)),
            dma((BANDS,)),
            dma((BANDS,)),
        ],
        compiler_params=pltpu.CompilerParams(
            collective_id=0, has_side_effects=True, vmem_limit_bytes=64 * 1024 * 1024
        ),
    )(tokens, qkv_weight.transpose(1, 0, 2), out_weight, head_kind)


def solution(mesh):
    return jax.shard_map(
        body,
        mesh=mesh,
        in_specs=(
            P(("frame", "band"), None),
            P("frame", None, "band"),
            P("frame", "band"),
            P("band"),
        ),
        out_specs=P(("frame", "band"), None),
        check_vma=False,
    )
```

time: 275 us -> 77.7 us (0.28)
  waiting for transfers between devices: 192 us -> 0 us
  Pallas kernels: 0 us -> 76 us
  blocking collectives: 29.8 us -> 0 us
  starting transfers between devices: 22 us -> 0 us
  between operations: 13.2 us -> 0.01 us
  local copies, waits for them, and re-layouts: 9.71 us -> 1.54 us
  matrix products: 6.73 us -> 0 us
    all_gather x2 -> x0, waiting for transfers between devices: 137 us -> none  [the longest x1 86.7 us: body(): weight_rows = lax.all_gather(out_weight, 'frame', axis=0, tiled=True)]
    pallas_call x0 -> x1, Pallas kernels: none -> 76 us  [body(): pl.pallas_call(kernel, out_shape=jax.ShapeDtypeStruct(tokens.shape, token...]
    reduce_scatter x1 -> x0, waiting for transfers between devices: 32.5 us -> none  [body(): lax.psum_scatter(jnp.dot(chosen, own_weight, preferred_element_type=jnp.f...]
    all_gather x1 -> x0, blocking collectives: 29.8 us -> none  [body(): frame_rows = lax.all_gather(tokens, 'band', axis=0, tiled=True)]
    all_to_all x3 -> x0, starting transfers between devices: 22 us -> none  [the longest x1 9.08 us: body(): lax.all_to_all(weight_rows, 'band', split_axis=0, concat_axis=1, tiled=True)]
    all_to_all x3 -> x0, waiting for transfers between devices: 21.4 us -> none  [the longest x1 10.9 us: body(): lax.all_to_all(packed, 'frame', split_axis=1, concat_axis=0, tiled=True)]
    all_gather x1 -> x0, local copies, waits for them, and re-layouts: 6.71 us -> none  [body(): full_weight = lax.all_gather(qkv_weight, 'frame', axis=0, tiled=True)]
    dot_general x6 -> x0, matrix products: 6.3 us -> none  [the longest x1 4.03 us: body(): jnp.dot(frame_rows, full_weight.reshape(full_weight.shape[0], columns), p...]
  transfers between devices with their start and end apart: 6 -> 0, of which waited for: 5 -> 0; matrix products, arithmetic and copies ran while one was open for 5% -> 0% of each run, Pallas kernels for 0% -> 0%
where the time goes in v1:
time: 77.7 us; the launch traced here: 77.5 us
  Pallas kernels  76 us (98%)
  local copies, waits for them, and re-layouts  1.54 us (2%)
    pallas_call x1, Pallas kernels, body(): pl.pallas_call(kernel, out_shape=jax.ShapeDtypeStruct(tokens.shape, token...  76 us

profile of v1, /device:TPU:1, one launch (start us, length us, event | category | flops | bytes accessed | tf_op | source)
XLA Modules:
  0.0 77.5 jit_solution(17569188727711036567)
XLA Ops:
  0.0 76.0 %shard_map.46 = bf16[16,3072]{1,0:T(8,128)(2,1)} custom-call(bf16[16,3072]{1,0:T(8,128)(2,1)} %tokens.1, bf16[3,48,256]{2,1,0:T(8,128)(2,1)} %bitcast.1, bf16[32,384]{1,0:T(8,128)(2,1)} %out_weight.1, s32[2]{0:T(128)} %kind_hbm.1), custom_call_target="tpu_custom_call" | custom-call | tf_op jit(solution)/shard_map/pallas_call | solution.py:568
  76.0 1.5 %copy.6 = bf16[16,3072]{1,0:T(8,128)(2,1)} copy(bf16[16,3072]{1,0:T(8,128)(2,1)} %shard_map.46) | data formatting | bytes 196608

commit v2 on v1

--- a/solution.py
+++ b/solution.py
@@ -253,10 +253,29 @@
         grid.begin(lambda first, second: wbuf.at[:, second, first, which])
 
     def token_along_x(which, block):
-        for step in (1, NX - 1, 2):
+        for step in (1, NX - 1):
             remote(
                 block, block, t_send.at[which, step], t_recv.at[which, step], (frame, band_at(step))
             ).start()
+
+    def token_passed_on(which, by):
+        if which == 0:
+            block = tbuf.at[odd, band_at(-by)]
+        else:
+            block = tbuf.at[other, 2 * wrap(x - by, NX) + which - 1]
+        remote(
+            block, block, t_send.at[which, 2], t_recv.at[which, 2], (frame, band_at(by))
+        ).start()
+
+    def token_to_sibling(hop):
+        from_band = band_at(-hop)
+        remote(
+            tbuf.at[odd, from_band],
+            tbuf.at[sibling_odd, from_band],
+            s_send.at[hop],
+            s_recv.at[hop],
+            sibling,
+        ).start()
 
     for copy in own:
         copy.wait()
@@ -356,19 +375,22 @@
 
         lax.fori_loop(0, PAIRS, one, 0)
 
+    for hop in (1, NX - 1):
+        await_bytes(tbuf.at[odd, band_at(-hop)], t_recv.at[0, hop])
+    token_passed_on(0, sign)
+    token_to_sibling(1)
+    token_to_sibling(NX - 1)
     ring_step(1)
     out_along_first(1)
-    for hop in (1, NX - 1, 2):
-        from_band = band_at(-hop)
-        await_bytes(tbuf.at[odd, from_band], t_recv.at[0, hop])
-        remote(
-            tbuf.at[odd, from_band],
-            tbuf.at[sibling_odd, from_band],
-            s_send.at[hop],
-            s_recv.at[hop],
-            sibling,
-        ).start()
+    for which, by in ((1, 1), (2, -1)):
+        for hop in (1, NX - 1):
+            await_bytes(
+                tbuf.at[other, 2 * wrap(x - hop, NX) + which - 1], t_recv.at[which, hop]
+            )
+        token_passed_on(which, by)
     ring_step(2)
+    await_bytes(tbuf.at[odd, band_at(2)], t_recv.at[0, 2])
+    token_to_sibling(2)
     out_along_first(2)
     ring_step(3)
     out_along_first(3)
@@ -377,7 +399,7 @@
     for hop in range(NX):
         from_band = 2 * wrap(x - hop, NX) + 1 - core
         await_bytes(tbuf.at[odd, from_band], s_recv.at[hop])
-        if hop:
+        if hop == 2:
             for which in range(2):
                 await_bytes(
                     tbuf.at[other, 2 * wrap(x - hop, NX) + which], t_recv.at[1 + which, hop]

time: 77.7 us -> 77.8 us (level)
  no operation moved by 1% of the time
where the time goes in v2:
time: 77.8 us; the launch traced here: 77.7 us
  Pallas kernels  76.1 us (98%)
  local copies, waits for them, and re-layouts  1.54 us (2%)
    pallas_call x1, Pallas kernels, body(): pl.pallas_call(kernel, out_shape=jax.ShapeDtypeStruct(tokens.shape, token...  76.1 us

profile of v2, /device:TPU:1, one launch (start us, length us, event | category | flops | bytes accessed | tf_op | source)
XLA Modules:
  0.0 77.7 jit_solution(16883490124680758152)
XLA Ops:
  0.0 76.1 %shard_map.46 = bf16[16,3072]{1,0:T(8,128)(2,1)} custom-call(bf16[16,3072]{1,0:T(8,128)(2,1)} %tokens.1, bf16[3,48,256]{2,1,0:T(8,128)(2,1)} %bitcast.1, bf16[32,384]{1,0:T(8,128)(2,1)} %out_weight.1, s32[2]{0:T(128)} %kind_hbm.1), custom_call_target="tpu_custom_call" | custom-call | tf_op jit(solution)/shard_map/pallas_call | solution.py:590
  76.1 1.5 %copy.6 = bf16[16,3072]{1,0:T(8,128)(2,1)} copy(bf16[16,3072]{1,0:T(8,128)(2,1)} %shard_map.46) | data formatting | bytes 196608

commit v3 on v2

--- a/solution.py
+++ b/solution.py
@@ -82,40 +82,33 @@
             self.device(self.first, there),
         ).start()
 
-    def begin(self, part):
-        own = part(self.first, self.second)
+    def begin(self, src, dst, device):
         for way in range(2):
-            if hops(self.n_second)[way]:
-                self.to_second(own, way, 0, 0)
-
-        for place in range(1, self.n_first // 2 + 1):
-            self.to_first(own, place, self.sign * wander(place))
-
-    def to_first(self, block, place, by):
-        there = wrap(self.first + by, self.n_first)
-        remote(
-            block,
-            block,
-            self.send.at[0, 0],
-            self.recv1.at[place],
-            self.device(there, self.second),
-        ).start()
+            there = wrap(self.second + self.turn(way), self.n_second)
+            remote(
+                src,
+                dst,
+                self.send.at[1, way],
+                self.recv2.at[way, 0, 0],
+                device(self.first, there),
+            ).start()
+        for place in range(1, self.n_first):
+            there = wrap(self.first + self.sign * wander(place), self.n_first)
+            remote(
+                src,
+                dst,
+                self.send.at[0, 0],
+                self.recv1.at[place],
+                device(there, self.second),
+            ).start()
 
     def along_first(self, place):
         block = self.block(
             wrap(self.first - self.sign * wander(place), self.n_first), self.second
         )
         await_bytes(block, self.recv1.at[place])
-        half = self.n_first // 4
-        if isinstance(place, int) and place == 2 * half - 1:
-            self.to_first(block, self.n_first - 1, self.sign * half)
-            if half > 1:
-                self.to_first(block, self.n_first - 3, self.sign)
-        if isinstance(place, int) and place == 2 * half and half > 1:
-            self.to_first(block, self.n_first - 2, -self.sign)
         for way in range(2):
-            if hops(self.n_second)[way]:
-                self.to_second(block, way, 0, place)
+            self.to_second(block, way, 0, place)
 
     def along_second(self, step, place):
         for way in range(2):
@@ -153,6 +146,7 @@
     by_frame,
     bias,
     kind,
+    cross,
     own_sem,
     z_send,
     z_recv,
@@ -207,10 +201,11 @@
 
     greet(sibling)
     greet((beside, sibling_band))
-    for step in (1, -1):
+    for step in range(1, NY):
         greet((y * NZ + wrap(z + step, NZ), band))
         greet((wrap(y + step, NY) * NZ + z, band))
-        greet((frame_at(along, 2 * wrap(pair + step, PAIRS) + odd), band))
+    for step in (1, -1):
+        greet((frame_at(wrap(along + step, NY), 2 * pair + other), band))
     for step in range(1, NX):
         greet((frame, band_at(step)))
 
@@ -223,22 +218,14 @@
         pltpu.make_async_copy(out_weight.at[16:32], obuf.at[1, z, y], own_sem.at[2]),
         pltpu.make_async_copy(tokens, tbuf.at[odd, band], own_sem.at[3]),
         pltpu.make_async_copy(kind_hbm, kind, own_sem.at[4]),
+        pltpu.make_async_copy(head_columns(other), cross, own_sem.at[5]),
     ]
     for copy in own:
         copy.start()
-    pl.semaphore_wait(barrier, 8 + NX - 1)
-
-    remote(
-        head_columns(other), wbuf.at[:, along, pair, odd], z_send.at[0], z_recv.at[0], (beside, band)
-    ).start()
-    beside_z = y * NZ + z + 1 - 2 * lax.rem(z, 2)
-    beside_y = (y + 1 - 2 * lax.rem(y, 2)) * NZ + z
-    remote(
-        tokens, tbuf.at[lax.rem(z, 2), band], z_send.at[1], z_recv.at[1 + core], (beside_z, 2 * x)
-    ).start()
-    remote(
-        tokens, tbuf.at[lax.rem(y, 2), band], z_send.at[2], z_recv.at[1 + core], (beside_y, 2 * x + 1)
-    ).start()
+    pl.semaphore_wait(barrier, 2 + NY - 1 + NZ - 1 + 2 + NX - 1)
+
+    for copy in own:
+        copy.wait()
 
     grid = Grid(
         lambda first, second: wbuf.at[:, second, first],
@@ -248,9 +235,6 @@
         sign,
         (w_send, w_recv1, w_recv2),
     )
-
-    def begin(which):
-        grid.begin(lambda first, second: wbuf.at[:, second, first, which])
 
     def token_along_x(which, block):
         for step in (1, NX - 1):
@@ -277,9 +261,20 @@
             sibling,
         ).start()
 
-    for copy in own:
-        copy.wait()
-    begin(odd)
+    here = wbuf.at[:, along, pair, odd]
+    grid.begin(here, here, grid.device)
+    grid.begin(
+        cross, here, lambda first, second: (frame_at(second, 2 * first + other), band)
+    )
+    remote(cross, here, z_send.at[0], z_recv.at[0], (beside, band)).start()
+    beside_z = y * NZ + z + 1 - 2 * lax.rem(z, 2)
+    beside_y = (y + 1 - 2 * lax.rem(y, 2)) * NZ + z
+    remote(
+        tokens, tbuf.at[lax.rem(z, 2), band], z_send.at[1], z_recv.at[1 + core], (beside_z, 2 * x)
+    ).start()
+    remote(
+        tokens, tbuf.at[lax.rem(y, 2), band], z_send.at[2], z_recv.at[1 + core], (beside_y, 2 * x + 1)
+    ).start()
     token_along_x(0, tbuf.at[odd, band])
     remote(
         tbuf.at[odd, band], tbuf.at[sibling_odd, band], s_send.at[0], s_recv.at[0], sibling
@@ -300,15 +295,10 @@
     by_frame[...] = jnp.where(tall == origin(wide), 1.0, 0.0).astype(jnp.bfloat16)
     bias[...] = jnp.where(lax.rem(tall, SHARE) == lax.rem(wide, SHARE), 0.0, -1e30)
 
-    await_bytes(wbuf.at[:, along, pair, other], z_recv.at[0])
-    begin(other)
     for which in range(2):
         await_bytes(tbuf.at[other, 2 * x + which], z_recv.at[1 + which])
         token_along_x(1 + which, tbuf.at[other, 2 * x + which])
 
-    def out_block(half, first, second):
-        return obuf.at[half, second, first]
-
     def out_here(half):
         return (z, y) if half == 0 else (y, z)
 
@@ -317,17 +307,6 @@
 
     def turn(way):
         return sign if way == 0 else -sign
-
-    def out_send1(half, way, step, block):
-        first, second = out_here(half)
-        there = wrap(first + turn(way), NY)
-        remote(
-            block,
-            block,
-            o_send.at[half, 0, way],
-            o_recv1.at[half, way, step],
-            out_device(half, there, second),
-        ).start()
 
     def out_send2(half, way, step, chunk):
         first, second = out_here(half)
@@ -340,17 +319,18 @@
             out_device(half, first, there),
         ).start()
 
-    def out_along_first(step):
+    def out_along_first():
         for half in range(2):
             first, second = out_here(half)
-            for way in range(2):
-                if step > hops(NY)[way]:
-                    continue
-                block = obuf.at[half, second, wrap(first - turn(way) * step, NY)]
-                if step:
-                    await_bytes(block, o_recv1.at[half, way, step - 1])
-                if step < hops(NY)[way]:
-                    out_send1(half, way, step, block)
+            block = obuf.at[half, second, first]
+            for step in range(1, NY):
+                remote(
+                    block,
+                    block,
+                    o_send.at[half, 0, 0],
+                    o_recv1.at[half],
+                    out_device(half, wrap(first + step, NY), second),
+                ).start()
 
     def out_along_second(step):
         for half in range(2):
@@ -364,7 +344,7 @@
                 if step < hops(NY)[way]:
                     out_send2(half, way, step, chunk)
 
-    out_along_first(0)
+    out_along_first()
     for place in range(1, PAIRS):
         grid.along_first(place)
 
@@ -375,27 +355,25 @@
 
         lax.fori_loop(0, PAIRS, one, 0)
 
+    ring_step(1)
     for hop in (1, NX - 1):
         await_bytes(tbuf.at[odd, band_at(-hop)], t_recv.at[0, hop])
     token_passed_on(0, sign)
     token_to_sibling(1)
     token_to_sibling(NX - 1)
-    ring_step(1)
-    out_along_first(1)
+    ring_step(2)
     for which, by in ((1, 1), (2, -1)):
         for hop in (1, NX - 1):
             await_bytes(
                 tbuf.at[other, 2 * wrap(x - hop, NX) + which - 1], t_recv.at[which, hop]
             )
         token_passed_on(which, by)
-    ring_step(2)
+    for half in range(2):
+        await_bytes(obuf.at[half, out_here(half)[1], 0 : NY - 1], o_recv1.at[half])
+    out_along_second(0)
     await_bytes(tbuf.at[odd, band_at(2)], t_recv.at[0, 2])
     token_to_sibling(2)
-    out_along_first(2)
     ring_step(3)
-    out_along_first(3)
-    out_along_first(4)
-    out_along_second(0)
     for hop in range(NX):
         from_band = 2 * wrap(x - hop, NX) + 1 - core
         await_bytes(tbuf.at[odd, from_band], s_recv.at[hop])
@@ -405,6 +383,8 @@
                     tbuf.at[other, 2 * wrap(x - hop, NX) + which], t_recv.at[1 + which, hop]
                 )
     ring_step(4)
+    await_bytes(wbuf.at[:, along, pair, other], z_recv.at[0])
+    out_along_second(1)
 
     chunk = 2 * NZ * DEPTH
 
@@ -461,7 +441,6 @@
         lax.fori_loop(1, PEERS, send, 0)
 
     exchange(0, msg, fin)
-    out_along_second(1)
     spatial = jnp.concatenate(
         [
             attend(
@@ -480,8 +459,7 @@
     await_bytes(wbuf.at[:, 0, 0 : PAIRS - 1], w_send.at[0, 0])
     for way in range(2):
         await_bytes(wbuf.at[:, 0 : hops(NY)[way]], w_send.at[1, way])
-        for half in range(2):
-            await_bytes(obuf.at[half, 0, 0 : hops(NY)[way]], o_send.at[half, 0, way])
+        await_bytes(obuf.at[way, 0, 0 : NY - 1], o_send.at[way, 0, 0])
     for hop in range(NX):
         await_bytes(tbuf.at[0, 0], s_send.at[hop])
         if hop:
@@ -609,14 +587,15 @@
             pltpu.VMEM((ROWS, ROWS), bf16),
             pltpu.VMEM((ROWS, ROWS), jnp.float32),
             pltpu.SMEM((2,), jnp.int32),
-            dma((5,)),
+            pltpu.VMEM((3, DEPTH, HEAD), bf16),
+            dma((6,)),
             dma((3,)),
             dma((3,)),
             dma((2, 2)),
             dma((4,)),
             dma((2, 4, 4)),
             dma((2, 2, 2)),
-            dma((2, 2, 4)),
+            dma((2,)),
             dma((2, 2, 4)),
             dma((3, NX)),
             dma((3, NX)),

time: 77.8 us -> 76.1 us (0.978)
  Pallas kernels: 76.1 us -> 74.4 us
    pallas_call x1, Pallas kernels: 76.1 us -> 74.4 us  [body(): pl.pallas_call(kernel, out_shape=jax.ShapeDtypeStruct(tokens.shape, token...]
where the time goes in v3:
time: 76.1 us; the launch traced here: 76 us
  Pallas kernels  74.4 us (98%)
  local copies, waits for them, and re-layouts  1.54 us (2%)
    pallas_call x1, Pallas kernels, body(): pl.pallas_call(kernel, out_shape=jax.ShapeDtypeStruct(tokens.shape, token...  74.4 us
    unnamed x1, local copies, waits for them, and re-layouts  1.54 us

profile of v3, /device:TPU:1, one launch (start us, length us, event | category | flops | bytes accessed | tf_op | source)
XLA Modules:
  0.0 76.0 jit_solution(2762802952493736350)
XLA Ops:
  0.0 74.4 %shard_map.46 = bf16[16,3072]{1,0:T(8,128)(2,1)} custom-call(bf16[16,3072]{1,0:T(8,128)(2,1)} %tokens.1, bf16[3,48,256]{2,1,0:T(8,128)(2,1)} %bitcast.1, bf16[32,384]{1,0:T(8,128)(2,1)} %out_weight.1, s32[2]{0:T(128)} %kind_hbm.1), custom_call_target="tpu_custom_call" | custom-call | tf_op jit(solution)/shard_map/pallas_call | solution.py:568
  74.5 1.5 %copy.6 = bf16[16,3072]{1,0:T(8,128)(2,1)} copy(bf16[16,3072]{1,0:T(8,128)(2,1)} %shard_map.46) | data formatting | bytes 196608

commit v4 on v3

--- a/solution.py
+++ b/solution.py
@@ -453,6 +453,8 @@
         ],
         axis=0,
     ).astype(jnp.bfloat16)
+    out_along_second(2)
+
     await_bytes(wbuf.at[:, 0, 0, 0], z_send.at[0])
     await_bytes(tbuf.at[0, 0], z_send.at[1])
     await_bytes(tbuf.at[0, 0], z_send.at[2])
@@ -466,14 +468,13 @@
             for which in range(3):
                 await_bytes(tbuf.at[0, 0], t_send.at[which, hop])
     await_bytes(fin, a_recv.at[0])
-    out_along_second(2)
     laid = fin[...].reshape(ROWS, 3 * HEAD)
     mixed = attend(laid[:, :HEAD], laid[:, HEAD : 2 * HEAD], laid[:, 2 * HEAD :], bias[...])
     rmsg[...] = mixed.reshape(rmsg.shape).astype(jnp.bfloat16)
     exchange(1, rmsg, rfin)
+    out_along_second(3)
     await_bytes(msg.at[0 : PEERS - 1], a_send.at[0])
     await_bytes(rfin, a_recv.at[1])
-    out_along_second(3)
     back = jnp.dot(
         by_frame[...], rfin[...].reshape(ROWS, HEAD), preferred_element_type=jnp.float32
     ).astype(jnp.bfloat16)

time: 76.1 us -> 76 us (level)
  no operation moved by 1% of the time
where the time goes in v4:
time: 76 us; the launch traced here: 75.8 us
  Pallas kernels  74.3 us (98%)
  local copies, waits for them, and re-layouts  1.54 us (2%)
    pallas_call x1, Pallas kernels, body(): pl.pallas_call(kernel, out_shape=jax.ShapeDtypeStruct(tokens.shape, token...  74.3 us
    unnamed x1, local copies, waits for them, and re-layouts  1.54 us

profile of v4, /device:TPU:1, one launch (start us, length us, event | category | flops | bytes accessed | tf_op | source)
XLA Modules:
  0.0 75.8 jit_solution(16124169610788429560)
XLA Ops:
  0.0 74.3 %shard_map.46 = bf16[16,3072]{1,0:T(8,128)(2,1)} custom-call(bf16[16,3072]{1,0:T(8,128)(2,1)} %tokens.1, bf16[3,48,256]{2,1,0:T(8,128)(2,1)} %bitcast.1, bf16[32,384]{1,0:T(8,128)(2,1)} %out_weight.1, s32[2]{0:T(128)} %kind_hbm.1), custom_call_target="tpu_custom_call" | custom-call | tf_op jit(solution)/shard_map/pallas_call | solution.py:569
  74.3 1.5 %copy.6 = bf16[16,3072]{1,0:T(8,128)(2,1)} copy(bf16[16,3072]{1,0:T(8,128)(2,1)} %shard_map.46) | data formatting | bytes 196608

commit v5 on v3

--- a/solution.py
+++ b/solution.py
@@ -280,21 +280,6 @@
         tbuf.at[odd, band], tbuf.at[sibling_odd, band], s_send.at[0], s_recv.at[0], sibling
     ).start()
 
-    tall = lax.broadcasted_iota(jnp.int32, (ROWS, ROWS), 0)
-    wide = lax.broadcasted_iota(jnp.int32, (ROWS, ROWS), 1)
-
-    def origin(row):
-        return (
-            lax.rem(lax.div(row, SHARE), 2) * POSITIONS
-            + lax.div(row, 2 * SHARE) * SHARE
-            + lax.rem(row, SHARE)
-        )
-
-    qkv_sum[...] = jnp.zeros_like(qkv_sum)
-    by_peer[...] = jnp.where(wide == origin(tall), 1.0, 0.0).astype(jnp.bfloat16)
-    by_frame[...] = jnp.where(tall == origin(wide), 1.0, 0.0).astype(jnp.bfloat16)
-    bias[...] = jnp.where(lax.rem(tall, SHARE) == lax.rem(wide, SHARE), 0.0, -1e30)
-
     for which in range(2):
         await_bytes(tbuf.at[other, 2 * x + which], z_recv.at[1 + which])
         token_along_x(1 + which, tbuf.at[other, 2 * x + which])
@@ -344,7 +329,6 @@
                 if step < hops(NY)[way]:
                     out_send2(half, way, step, chunk)
 
-    out_along_first()
     for place in range(1, PAIRS):
         grid.along_first(place)
 
@@ -356,6 +340,7 @@
         lax.fori_loop(0, PAIRS, one, 0)
 
     ring_step(1)
+    out_along_first()
     for hop in (1, NX - 1):
         await_bytes(tbuf.at[odd, band_at(-hop)], t_recv.at[0, hop])
     token_passed_on(0, sign)
@@ -368,12 +353,25 @@
                 tbuf.at[other, 2 * wrap(x - hop, NX) + which - 1], t_recv.at[which, hop]
             )
         token_passed_on(which, by)
-    for half in range(2):
-        await_bytes(obuf.at[half, out_here(half)[1], 0 : NY - 1], o_recv1.at[half])
-    out_along_second(0)
     await_bytes(tbuf.at[odd, band_at(2)], t_recv.at[0, 2])
     token_to_sibling(2)
     ring_step(3)
+
+    tall = lax.broadcasted_iota(jnp.int32, (ROWS, ROWS), 0)
+    wide = lax.broadcasted_iota(jnp.int32, (ROWS, ROWS), 1)
+
+    def origin(row):
+        return (
+            lax.rem(lax.div(row, SHARE), 2) * POSITIONS
+            + lax.div(row, 2 * SHARE) * SHARE
+            + lax.rem(row, SHARE)
+        )
+
+    qkv_sum[...] = jnp.zeros_like(qkv_sum)
+    by_peer[...] = jnp.where(wide == origin(tall), 1.0, 0.0).astype(jnp.bfloat16)
+    by_frame[...] = jnp.where(tall == origin(wide), 1.0, 0.0).astype(jnp.bfloat16)
+    bias[...] = jnp.where(lax.rem(tall, SHARE) == lax.rem(wide, SHARE), 0.0, -1e30)
+
     for hop in range(NX):
         from_band = 2 * wrap(x - hop, NX) + 1 - core
         await_bytes(tbuf.at[odd, from_band], s_recv.at[hop])
@@ -384,7 +382,9 @@
                 )
     ring_step(4)
     await_bytes(wbuf.at[:, along, pair, other], z_recv.at[0])
-    out_along_second(1)
+    for half in range(2):
+        await_bytes(obuf.at[half, out_here(half)[1], 0 : NY - 1], o_recv1.at[half])
+    out_along_second(0)
 
     chunk = 2 * NZ * DEPTH
 
@@ -453,6 +453,8 @@
         ],
         axis=0,
     ).astype(jnp.bfloat16)
+    out_along_second(1)
+
     await_bytes(wbuf.at[:, 0, 0, 0], z_send.at[0])
     await_bytes(tbuf.at[0, 0], z_send.at[1])
     await_bytes(tbuf.at[0, 0], z_send.at[2])

time: 76.1 us -> 77.1 us (1.013)
  Pallas kernels: 74.4 us -> 75.4 us
    pallas_call x1, Pallas kernels: 74.4 us -> 75.4 us  [body(): pl.pallas_call(kernel, out_shape=jax.ShapeDtypeStruct(tokens.shape, token...]
where the time goes in v5:
time: 77.1 us; the launch traced here: 77 us
  Pallas kernels  75.4 us (98%)
  local copies, waits for them, and re-layouts  1.54 us (2%)
    pallas_call x1, Pallas kernels, body(): pl.pallas_call(kernel, out_shape=jax.ShapeDtypeStruct(tokens.shape, token...  75.4 us

profile of v5, /device:TPU:1, one launch (start us, length us, event | category | flops | bytes accessed | tf_op | source)
XLA Modules:
  0.0 77.0 jit_solution(18357400009153766234)
XLA Ops:
  0.0 75.4 %shard_map.46 = bf16[16,3072]{1,0:T(8,128)(2,1)} custom-call(bf16[16,3072]{1,0:T(8,128)(2,1)} %tokens.1, bf16[3,48,256]{2,1,0:T(8,128)(2,1)} %bitcast.1, bf16[32,384]{1,0:T(8,128)(2,1)} %out_weight.1, s32[2]{0:T(128)} %kind_hbm.1), custom_call_target="tpu_custom_call" | custom-call | tf_op jit(solution)/shard_map/pallas_call | solution.py:570
  75.4 1.5 %copy.6 = bf16[16,3072]{1,0:T(8,128)(2,1)} copy(bf16[16,3072]{1,0:T(8,128)(2,1)} %shard_map.46) | data formatting | bytes 196608

commit v6 on v4

--- a/solution.py
+++ b/solution.py
@@ -69,11 +69,12 @@
         self.sign = sign
         self.send, self.recv1, self.recv2 = sems
 
-    def turn(self, way):
-        return self.sign if way == 0 else -self.sign
-
-    def to_second(self, block, way, step, place):
-        there = wrap(self.second + self.turn(way), self.n_second)
+    def turn(self, way, place):
+        flip = 1 - 2 * (place // 2 if isinstance(place, int) else lax.div(place, 2))
+        return (self.sign if way == 0 else -self.sign) * flip
+
+    def to_second(self, block, way, step, place, by=1):
+        there = wrap(self.second + by * self.turn(way, place), self.n_second)
         remote(
             block,
             block,
@@ -84,7 +85,7 @@
 
     def begin(self, src, dst, device):
         for way in range(2):
-            there = wrap(self.second + self.turn(way), self.n_second)
+            there = wrap(self.second + self.turn(way, 0), self.n_second)
             remote(
                 src,
                 dst,
@@ -112,16 +113,17 @@
 
     def along_second(self, step, place):
         for way in range(2):
-            count = hops(self.n_second)[way]
-            if step > count:
+            if step > hops(self.n_second)[way]:
                 continue
             block = self.block(
                 wrap(self.first - self.sign * wander(place), self.n_first),
-                wrap(self.second - self.turn(way) * step, self.n_second),
+                wrap(self.second - self.turn(way, place) * step, self.n_second),
             )
             await_bytes(block, self.recv2.at[way, step - 1, place])
-            if step < count:
+            if step < 3:
                 self.to_second(block, way, step, place)
+            if step == 2 and way == 0:
+                self.to_second(block, way, 3, place, 2)
 
 
 def kernel(
@@ -431,14 +433,14 @@
 
     def exchange(stage, source, target):
         def send(step, carry):
-            there = lax.rem(me + step, PEERS)
+            there = lax.rem(me + PEERS // 2 + wander(step) + PEERS, PEERS)
             remote(
                 source.at[there], target.at[me], a_send.at[stage], a_recv.at[stage], peer(there)
             ).start()
             return carry
 
         pltpu.make_async_copy(source.at[me], target.at[me], a_recv.at[stage]).start()
-        lax.fori_loop(1, PEERS, send, 0)
+        lax.fori_loop(0, PEERS - 1, send, 0)
 
     exchange(0, msg, fin)
     spatial = jnp.concatenate(
@@ -481,21 +483,13 @@
     temporal = jnp.full((ROWS, HEAD), kind[odd], jnp.int32) == 1
     cbuf[...] = jnp.where(temporal, back, spatial).reshape(cbuf.shape)
 
-    for step in (1, NX - 1, 2):
+    for which, step in ((1, 2), (1, 1), (1, NX - 1), (0, 2), (1, 0), (0, 1), (0, NX - 1)):
         remote(
-            cbuf.at[odd],
+            cbuf.at[odd if which == 0 else other],
             mbuf.at[band, odd],
-            m_send.at[0, step],
-            m_recv.at[0, step],
-            (frame, band_at(step)),
-        ).start()
-    for step in (1, NX - 1, 2, 0):
-        remote(
-            cbuf.at[other],
-            mbuf.at[band, odd],
-            m_send.at[1, step],
-            m_recv.at[1, step],
-            (beside, band_at(step)),
+            m_send.at[which, step],
+            m_recv.at[which, step],
+            (frame if which == 0 else beside, band_at(step)),
         ).start()
     remote(
         cbuf.at[odd], mbuf.at[band, odd], n_send.at[0, 0], n_recv.at[0, 0], sibling

time: 76 us -> 74.8 us (0.984)
  Pallas kernels: 74.3 us -> 73.1 us
    pallas_call x1, Pallas kernels: 74.3 us -> 73.1 us  [body(): pl.pallas_call(kernel, out_shape=jax.ShapeDtypeStruct(tokens.shape, token...]
where the time goes in v6:
time: 74.8 us; the launch traced here: 74.6 us
  Pallas kernels  73.1 us (98%)
  local copies, waits for them, and re-layouts  1.54 us (2%)
    pallas_call x1, Pallas kernels, body(): pl.pallas_call(kernel, out_shape=jax.ShapeDtypeStruct(tokens.shape, token...  73.1 us
    unnamed x1, local copies, waits for them, and re-layouts  1.54 us

profile of v6, /device:TPU:1, one launch (start us, length us, event | category | flops | bytes accessed | tf_op | source)
XLA Modules:
  0.0 74.6 jit_solution(16157127653360235955)
XLA Ops:
  0.0 73.1 %shard_map.46 = bf16[16,3072]{1,0:T(8,128)(2,1)} custom-call(bf16[16,3072]{1,0:T(8,128)(2,1)} %tokens.1, bf16[3,48,256]{2,1,0:T(8,128)(2,1)} %bitcast.1, bf16[32,384]{1,0:T(8,128)(2,1)} %out_weight.1, s32[2]{0:T(128)} %kind_hbm.1), custom_call_target="tpu_custom_call" | custom-call | tf_op jit(solution)/shard_map/pallas_call | solution.py:563
  73.1 1.5 %copy.6 = bf16[16,3072]{1,0:T(8,128)(2,1)} copy(bf16[16,3072]{1,0:T(8,128)(2,1)} %shard_map.46) | data formatting | bytes 196608

commit v7 on v6

--- a/solution.py
+++ b/solution.py
@@ -310,9 +310,9 @@
     def turn(way):
         return sign if way == 0 else -sign
 
-    def out_send2(half, way, step, chunk):
+    def out_send2(half, way, step, chunk, by=1):
         first, second = out_here(half)
-        there = wrap(second + turn(way), NY)
+        there = wrap(second + by * turn(way), NY)
         remote(
             chunk,
             chunk,
@@ -343,8 +343,10 @@
                 chunk = obuf.at[half, wrap(second - turn(way) * step, NY)]
                 if step:
                     await_bytes(chunk, o_recv2.at[half, way, step - 1])
-                if step < hops(NY)[way]:
+                if step < 3:
                     out_send2(half, way, step, chunk)
+                if step == 2 and way == 0:
+                    out_send2(half, way, 3, chunk, 2)
 
     out_along_first()
     for place in range(1, PAIRS):
@@ -370,9 +372,6 @@
                 tbuf.at[other, 2 * wrap(x - hop, NX) + which - 1], t_recv.at[which, hop]
             )
         token_passed_on(which, by)
-    for half in range(2):
-        await_bytes(obuf.at[half, out_here(half)[1], 0 : NY - 1], o_recv1.at[half])
-    out_along_second(0)
     await_bytes(tbuf.at[odd, band_at(2)], t_recv.at[0, 2])
     token_to_sibling(2)
     ring_step(3)
@@ -386,7 +385,9 @@
                 )
     ring_step(4)
     await_bytes(wbuf.at[:, along, pair, other], z_recv.at[0])
-    out_along_second(1)
+    for half in range(2):
+        await_bytes(obuf.at[half, out_here(half)[1], 0 : NY - 1], o_recv1.at[half])
+    out_along_second(0)
 
     chunk = 2 * NZ * DEPTH
 
@@ -455,7 +456,7 @@
         ],
         axis=0,
     ).astype(jnp.bfloat16)
-    out_along_second(2)
+    out_along_second(1)
 
     await_bytes(wbuf.at[:, 0, 0, 0], z_send.at[0])
     await_bytes(tbuf.at[0, 0], z_send.at[1])
@@ -474,7 +475,7 @@
     mixed = attend(laid[:, :HEAD], laid[:, HEAD : 2 * HEAD], laid[:, 2 * HEAD :], bias[...])
     rmsg[...] = mixed.reshape(rmsg.shape).astype(jnp.bfloat16)
     exchange(1, rmsg, rfin)
-    out_along_second(3)
+    out_along_second(2)
     await_bytes(msg.at[0 : PEERS - 1], a_send.at[0])
     await_bytes(rfin, a_recv.at[1])
     back = jnp.dot(
@@ -500,6 +501,7 @@
         block = mbuf.at[band_at(-hop), odd if which == 0 else other]
         await_bytes(block, m_recv.at[which, hop])
         remote(block, block, n_send.at[which, hop], n_recv.at[which, hop], sibling).start()
+    out_along_second(3)
     out_along_second(4)
     last.wait()
 

time: 74.8 us -> 73 us (0.976)
  Pallas kernels: 73.1 us -> 71.3 us
    pallas_call x1, Pallas kernels: 73.1 us -> 71.3 us  [body(): pl.pallas_call(kernel, out_shape=jax.ShapeDtypeStruct(tokens.shape, token...]
where the time goes in v7:
time: 73 us; the launch traced here: 72.9 us
  Pallas kernels  71.3 us (98%)
  local copies, waits for them, and re-layouts  1.54 us (2%)
    pallas_call x1, Pallas kernels, body(): pl.pallas_call(kernel, out_shape=jax.ShapeDtypeStruct(tokens.shape, token...  71.3 us
    unnamed x1, local copies, waits for them, and re-layouts  1.54 us

profile of v7, /device:TPU:1, one launch (start us, length us, event | category | flops | bytes accessed | tf_op | source)
XLA Modules:
  0.0 72.9 jit_solution(8535914506624741558)
XLA Ops:
  0.0 71.3 %shard_map.46 = bf16[16,3072]{1,0:T(8,128)(2,1)} custom-call(bf16[16,3072]{1,0:T(8,128)(2,1)} %tokens.1, bf16[3,48,256]{2,1,0:T(8,128)(2,1)} %bitcast.1, bf16[32,384]{1,0:T(8,128)(2,1)} %out_weight.1, s32[2]{0:T(128)} %kind_hbm.1), custom_call_target="tpu_custom_call" | custom-call | tf_op jit(solution)/shard_map/pallas_call | solution.py:565
  71.3 1.5 %copy.6 = bf16[16,3072]{1,0:T(8,128)(2,1)} copy(bf16[16,3072]{1,0:T(8,128)(2,1)} %shard_map.46) | data formatting | bytes 196608

commit v8 on v7

--- a/solution.py
+++ b/solution.py
@@ -297,10 +297,6 @@
     by_frame[...] = jnp.where(tall == origin(wide), 1.0, 0.0).astype(jnp.bfloat16)
     bias[...] = jnp.where(lax.rem(tall, SHARE) == lax.rem(wide, SHARE), 0.0, -1e30)
 
-    for which in range(2):
-        await_bytes(tbuf.at[other, 2 * x + which], z_recv.at[1 + which])
-        token_along_x(1 + which, tbuf.at[other, 2 * x + which])
-
     def out_here(half):
         return (z, y) if half == 0 else (y, z)
 
@@ -348,24 +344,27 @@
                 if step == 2 and way == 0:
                     out_send2(half, way, 3, chunk, 2)
 
-    out_along_first()
-    for place in range(1, PAIRS):
-        grid.along_first(place)
-
-    def ring_step(step):
+    def ring_step(step, start):
         def one(place, carry):
             grid.along_second(step, place)
             return carry
 
-        lax.fori_loop(0, PAIRS, one, 0)
-
-    ring_step(1)
+        lax.fori_loop(start, PAIRS, one, 0)
+
+    grid.along_second(1, 0)
+    for place in range(1, PAIRS):
+        grid.along_first(place)
+    grid.along_second(2, 0)
+    for which in range(2):
+        await_bytes(tbuf.at[other, 2 * x + which], z_recv.at[1 + which])
+        token_along_x(1 + which, tbuf.at[other, 2 * x + which])
+    ring_step(1, 1)
     for hop in (1, NX - 1):
         await_bytes(tbuf.at[odd, band_at(-hop)], t_recv.at[0, hop])
     token_passed_on(0, sign)
     token_to_sibling(1)
     token_to_sibling(NX - 1)
-    ring_step(2)
+    ring_step(2, 1)
     for which, by in ((1, 1), (2, -1)):
         for hop in (1, NX - 1):
             await_bytes(
@@ -374,7 +373,8 @@
         token_passed_on(which, by)
     await_bytes(tbuf.at[odd, band_at(2)], t_recv.at[0, 2])
     token_to_sibling(2)
-    ring_step(3)
+    out_along_first()
+    ring_step(3, 0)
     for hop in range(NX):
         from_band = 2 * wrap(x - hop, NX) + 1 - core
         await_bytes(tbuf.at[odd, from_band], s_recv.at[hop])
@@ -383,11 +383,8 @@
                 await_bytes(
                     tbuf.at[other, 2 * wrap(x - hop, NX) + which], t_recv.at[1 + which, hop]
                 )
-    ring_step(4)
+    ring_step(4, 0)
     await_bytes(wbuf.at[:, along, pair, other], z_recv.at[0])
-    for half in range(2):
-        await_bytes(obuf.at[half, out_here(half)[1], 0 : NY - 1], o_recv1.at[half])
-    out_along_second(0)
 
     chunk = 2 * NZ * DEPTH
 
@@ -444,6 +441,9 @@
         lax.fori_loop(0, PEERS - 1, send, 0)
 
     exchange(0, msg, fin)
+    for half in range(2):
+        await_bytes(obuf.at[half, out_here(half)[1], 0 : NY - 1], o_recv1.at[half])
+    out_along_second(0)
     spatial = jnp.concatenate(
         [
             attend(
@@ -456,8 +456,6 @@
         ],
         axis=0,
     ).astype(jnp.bfloat16)
-    out_along_second(1)
-
     await_bytes(wbuf.at[:, 0, 0, 0], z_send.at[0])
     await_bytes(tbuf.at[0, 0], z_send.at[1])
     await_bytes(tbuf.at[0, 0], z_send.at[2])
@@ -471,13 +469,14 @@
             for which in range(3):
                 await_bytes(tbuf.at[0, 0], t_send.at[which, hop])
     await_bytes(fin, a_recv.at[0])
+    out_along_second(1)
     laid = fin[...].reshape(ROWS, 3 * HEAD)
     mixed = attend(laid[:, :HEAD], laid[:, HEAD : 2 * HEAD], laid[:, 2 * HEAD :], bias[...])
     rmsg[...] = mixed.reshape(rmsg.shape).astype(jnp.bfloat16)
     exchange(1, rmsg, rfin)
-    out_along_second(2)
     await_bytes(msg.at[0 : PEERS - 1], a_send.at[0])
     await_bytes(rfin, a_recv.at[1])
+    out_along_second(2)
     back = jnp.dot(
         by_frame[...], rfin[...].reshape(ROWS, HEAD), preferred_element_type=jnp.float32
     ).astype(jnp.bfloat16)

time: 73 us -> 74.8 us (1.025)
  Pallas kernels: 71.3 us -> 73.1 us
    pallas_call x1, Pallas kernels: 71.3 us -> 73.1 us  [body(): pl.pallas_call(kernel, out_shape=jax.ShapeDtypeStruct(tokens.shape, token...]
where the time goes in v8:
time: 74.8 us; the launch traced here: 74.7 us
  Pallas kernels  73.1 us (98%)
  local copies, waits for them, and re-layouts  1.54 us (2%)
    pallas_call x1, Pallas kernels, body(): pl.pallas_call(kernel, out_shape=jax.ShapeDtypeStruct(tokens.shape, token...  73.1 us
    unnamed x1, local copies, waits for them, and re-layouts  1.54 us

profile of v8, /device:TPU:1, one launch (start us, length us, event | category | flops | bytes accessed | tf_op | source)
XLA Modules:
  0.0 74.7 jit_solution(5320974335991616781)
XLA Ops:
  0.0 73.1 %shard_map.46 = bf16[16,3072]{1,0:T(8,128)(2,1)} custom-call(bf16[16,3072]{1,0:T(8,128)(2,1)} %tokens.1, bf16[3,48,256]{2,1,0:T(8,128)(2,1)} %bitcast.1, bf16[32,384]{1,0:T(8,128)(2,1)} %out_weight.1, s32[2]{0:T(128)} %kind_hbm.1), custom_call_target="tpu_custom_call" | custom-call | tf_op jit(solution)/shard_map/pallas_call | solution.py:564
  73.1 1.5 %copy.6 = bf16[16,3072]{1,0:T(8,128)(2,1)} copy(bf16[16,3072]{1,0:T(8,128)(2,1)} %shard_map.46) | data formatting | bytes 196608

commit v9 on v8

--- a/solution.py
+++ b/solution.py
@@ -351,6 +351,7 @@
 
         lax.fori_loop(start, PAIRS, one, 0)
 
+    out_along_first()
     grid.along_second(1, 0)
     for place in range(1, PAIRS):
         grid.along_first(place)
@@ -373,7 +374,6 @@
         token_passed_on(which, by)
     await_bytes(tbuf.at[odd, band_at(2)], t_recv.at[0, 2])
     token_to_sibling(2)
-    out_along_first()
     ring_step(3, 0)
     for hop in range(NX):
         from_band = 2 * wrap(x - hop, NX) + 1 - core
@@ -384,6 +384,9 @@
                     tbuf.at[other, 2 * wrap(x - hop, NX) + which], t_recv.at[1 + which, hop]
                 )
     ring_step(4, 0)
+    for half in range(2):
+        await_bytes(obuf.at[half, out_here(half)[1], 0 : NY - 1], o_recv1.at[half])
+    out_along_second(0)
     await_bytes(wbuf.at[:, along, pair, other], z_recv.at[0])
 
     chunk = 2 * NZ * DEPTH
@@ -441,9 +444,6 @@
         lax.fori_loop(0, PEERS - 1, send, 0)
 
     exchange(0, msg, fin)
-    for half in range(2):
-        await_bytes(obuf.at[half, out_here(half)[1], 0 : NY - 1], o_recv1.at[half])
-    out_along_second(0)
     spatial = jnp.concatenate(
         [
             attend(
@@ -456,6 +456,8 @@
         ],
         axis=0,
     ).astype(jnp.bfloat16)
+    out_along_second(1)
+
     await_bytes(wbuf.at[:, 0, 0, 0], z_send.at[0])
     await_bytes(tbuf.at[0, 0], z_send.at[1])
     await_bytes(tbuf.at[0, 0], z_send.at[2])
@@ -469,14 +471,13 @@
             for which in range(3):
                 await_bytes(tbuf.at[0, 0], t_send.at[which, hop])
     await_bytes(fin, a_recv.at[0])
-    out_along_second(1)
     laid = fin[...].reshape(ROWS, 3 * HEAD)
     mixed = attend(laid[:, :HEAD], laid[:, HEAD : 2 * HEAD], laid[:, 2 * HEAD :], bias[...])
     rmsg[...] = mixed.reshape(rmsg.shape).astype(jnp.bfloat16)
     exchange(1, rmsg, rfin)
+    out_along_second(2)
     await_bytes(msg.at[0 : PEERS - 1], a_send.at[0])
     await_bytes(rfin, a_recv.at[1])
-    out_along_second(2)
     back = jnp.dot(
         by_frame[...], rfin[...].reshape(ROWS, HEAD), preferred_element_type=jnp.float32
     ).astype(jnp.bfloat16)

time: 74.8 us -> 74.2 us (level)
  no operation moved by 1% of the time
where the time goes in v9:
time: 74.2 us; the launch traced here: 74 us
  Pallas kernels  72.5 us (98%)
  local copies, waits for them, and re-layouts  1.54 us (2%)
    pallas_call x1, Pallas kernels, body(): pl.pallas_call(kernel, out_shape=jax.ShapeDtypeStruct(tokens.shape, token...  72.5 us
    unnamed x1, local copies, waits for them, and re-layouts  1.54 us

profile of v9, /device:TPU:1, one launch (start us, length us, event | category | flops | bytes accessed | tf_op | source)
XLA Modules:
  0.0 74.0 jit_solution(13266412257834076905)
XLA Ops:
  0.0 72.5 %shard_map.46 = bf16[16,3072]{1,0:T(8,128)(2,1)} custom-call(bf16[16,3072]{1,0:T(8,128)(2,1)} %tokens.1, bf16[3,48,256]{2,1,0:T(8,128)(2,1)} %bitcast.1, bf16[32,384]{1,0:T(8,128)(2,1)} %out_weight.1, s32[2]{0:T(128)} %kind_hbm.1), custom_call_target="tpu_custom_call" | custom-call | tf_op jit(solution)/shard_map/pallas_call | solution.py:565
  72.5 1.5 %copy.6 = bf16[16,3072]{1,0:T(8,128)(2,1)} copy(bf16[16,3072]{1,0:T(8,128)(2,1)} %shard_map.46) | data formatting | bytes 196608

commit v10 on v7

--- a/solution.py
+++ b/solution.py
@@ -297,6 +297,7 @@
     by_frame[...] = jnp.where(tall == origin(wide), 1.0, 0.0).astype(jnp.bfloat16)
     bias[...] = jnp.where(lax.rem(tall, SHARE) == lax.rem(wide, SHARE), 0.0, -1e30)
 
+    grid.along_second(1, 0)
     for which in range(2):
         await_bytes(tbuf.at[other, 2 * x + which], z_recv.at[1 + which])
         token_along_x(1 + which, tbuf.at[other, 2 * x + which])
@@ -352,20 +353,21 @@
     for place in range(1, PAIRS):
         grid.along_first(place)
 
-    def ring_step(step):
+    def ring_step(step, start):
         def one(place, carry):
             grid.along_second(step, place)
             return carry
 
-        lax.fori_loop(0, PAIRS, one, 0)
-
-    ring_step(1)
+        lax.fori_loop(start, PAIRS, one, 0)
+
+    grid.along_second(2, 0)
+    ring_step(1, 1)
     for hop in (1, NX - 1):
         await_bytes(tbuf.at[odd, band_at(-hop)], t_recv.at[0, hop])
     token_passed_on(0, sign)
     token_to_sibling(1)
     token_to_sibling(NX - 1)
-    ring_step(2)
+    ring_step(2, 1)
     for which, by in ((1, 1), (2, -1)):
         for hop in (1, NX - 1):
             await_bytes(
@@ -374,7 +376,7 @@
         token_passed_on(which, by)
     await_bytes(tbuf.at[odd, band_at(2)], t_recv.at[0, 2])
     token_to_sibling(2)
-    ring_step(3)
+    ring_step(3, 0)
     for hop in range(NX):
         from_band = 2 * wrap(x - hop, NX) + 1 - core
         await_bytes(tbuf.at[odd, from_band], s_recv.at[hop])
@@ -383,7 +385,7 @@
                 await_bytes(
                     tbuf.at[other, 2 * wrap(x - hop, NX) + which], t_recv.at[1 + which, hop]
                 )
-    ring_step(4)
+    ring_step(4, 0)
     await_bytes(wbuf.at[:, along, pair, other], z_recv.at[0])
     for half in range(2):
         await_bytes(obuf.at[half, out_here(half)[1], 0 : NY - 1], o_recv1.at[half])

time: 73 us -> 74.2 us (1.016)
  Pallas kernels: 71.3 us -> 72.5 us
    pallas_call x1, Pallas kernels: 71.3 us -> 72.5 us  [body(): pl.pallas_call(kernel, out_shape=jax.ShapeDtypeStruct(tokens.shape, token...]
where the time goes in v10:
time: 74.2 us; the launch traced here: 74.1 us
  Pallas kernels  72.5 us (98%)
  local copies, waits for them, and re-layouts  1.54 us (2%)
    pallas_call x1, Pallas kernels, body(): pl.pallas_call(kernel, out_shape=jax.ShapeDtypeStruct(tokens.shape, token...  72.5 us
    unnamed x1, local copies, waits for them, and re-layouts  1.54 us

profile of v10, /device:TPU:1, one launch (start us, length us, event | category | flops | bytes accessed | tf_op | source)
XLA Modules:
  0.0 74.1 jit_solution(8239580999757785667)
XLA Ops:
  0.0 72.5 %shard_map.46 = bf16[16,3072]{1,0:T(8,128)(2,1)} custom-call(bf16[16,3072]{1,0:T(8,128)(2,1)} %tokens.1, bf16[3,48,256]{2,1,0:T(8,128)(2,1)} %bitcast.1, bf16[32,384]{1,0:T(8,128)(2,1)} %out_weight.1, s32[2]{0:T(128)} %kind_hbm.1), custom_call_target="tpu_custom_call" | custom-call | tf_op jit(solution)/shard_map/pallas_call | solution.py:567
  72.5 1.5 %copy.6 = bf16[16,3072]{1,0:T(8,128)(2,1)} copy(bf16[16,3072]{1,0:T(8,128)(2,1)} %shard_map.46) | data formatting | bytes 196608

commit v11 on v7

--- a/solution.py
+++ b/solution.py
@@ -196,21 +196,6 @@
     def peer(index):
         return (frame_at(lax.div(index, PAIRS), 2 * lax.rem(index, PAIRS) + odd), band)
 
-    barrier = pltpu.get_barrier_semaphore()
-
-    def greet(device):
-        pl.semaphore_signal(barrier, inc=1, device_id=device, device_id_type=MESH)
-
-    greet(sibling)
-    greet((beside, sibling_band))
-    for step in range(1, NY):
-        greet((y * NZ + wrap(z + step, NZ), band))
-        greet((wrap(y + step, NY) * NZ + z, band))
-    for step in (1, -1):
-        greet((frame_at(wrap(along + step, NY), 2 * pair + other), band))
-    for step in range(1, NX):
-        greet((frame, band_at(step)))
-
     def head_columns(which):
         return qkv.at[:, :, pl.ds(pl.multiple_of(which * HEAD, HEAD), HEAD)]
 
@@ -224,10 +209,26 @@
     ]
     for copy in own:
         copy.start()
+
+    barrier = pltpu.get_barrier_semaphore()
+
+    def greet(device):
+        pl.semaphore_signal(barrier, inc=1, device_id=device, device_id_type=MESH)
+
+    greet(sibling)
+    greet((beside, sibling_band))
+    for step in range(1, NY):
+        greet((y * NZ + wrap(z + step, NZ), band))
+        greet((wrap(y + step, NY) * NZ + z, band))
+    for step in (1, -1):
+        greet((frame_at(wrap(along + step, NY), 2 * pair + other), band))
+    for step in range(1, NX):
+        greet((frame, band_at(step)))
+
     pl.semaphore_wait(barrier, 2 + NY - 1 + NZ - 1 + 2 + NX - 1)
 
-    for copy in own:
-        copy.wait()
+    own[0].wait()
+    own[5].wait()
 
     grid = Grid(
         lambda first, second: wbuf.at[:, second, first],
@@ -277,6 +278,8 @@
     remote(
         tokens, tbuf.at[lax.rem(y, 2), band], z_send.at[2], z_recv.at[1 + core], (beside_y, 2 * x + 1)
     ).start()
+    for copy in own[1:5]:
+        copy.wait()
     token_along_x(0, tbuf.at[odd, band])
     remote(
         tbuf.at[odd, band], tbuf.at[sibling_odd, band], s_send.at[0], s_recv.at[0], sibling
@@ -321,18 +324,35 @@
             out_device(half, first, there),
         ).start()
 
+    def out_to_first(half, block, by, sem):
+        first, second = out_here(half)
+        remote(
+            block,
+            block,
+            o_send.at[half, 0, 0],
+            o_recv1.at[half, sem],
+            out_device(half, wrap(first + by, NY), second),
+        ).start()
+
     def out_along_first():
         for half in range(2):
             first, second = out_here(half)
             block = obuf.at[half, second, first]
-            for step in range(1, NY):
-                remote(
-                    block,
-                    block,
-                    o_send.at[half, 0, 0],
-                    o_recv1.at[half],
-                    out_device(half, wrap(first + step, NY), second),
-                ).start()
+            out_to_first(half, block, 2 * sign, 0)
+            out_to_first(half, block, -2 * sign, 1)
+            out_to_first(half, block, sign, 2)
+            out_to_first(half, block, -sign, 2)
+
+    def out_beyond():
+        for half in range(2):
+            first, second = out_here(half)
+            block = obuf.at[half, second, wrap(first - 2 * sign, NY)]
+            await_bytes(block, o_recv1.at[half, 0])
+            out_to_first(half, block, 2 * sign, 2)
+            out_to_first(half, block, sign, 2)
+            block = obuf.at[half, second, wrap(first + 2 * sign, NY)]
+            await_bytes(block, o_recv1.at[half, 1])
+            out_to_first(half, block, -sign, 2)
 
     def out_along_second(step):
         for half in range(2):
@@ -360,6 +380,7 @@
         lax.fori_loop(0, PAIRS, one, 0)
 
     ring_step(1)
+    out_beyond()
     for hop in (1, NX - 1):
         await_bytes(tbuf.at[odd, band_at(-hop)], t_recv.at[0, hop])
     token_passed_on(0, sign)
@@ -386,7 +407,7 @@
     ring_step(4)
     await_bytes(wbuf.at[:, along, pair, other], z_recv.at[0])
     for half in range(2):
-        await_bytes(obuf.at[half, out_here(half)[1], 0 : NY - 1], o_recv1.at[half])
+        await_bytes(obuf.at[half, out_here(half)[1], 0 : NY - 3], o_recv1.at[half, 2])
     out_along_second(0)
 
     chunk = 2 * NZ * DEPTH
@@ -592,7 +613,7 @@
             dma((4,)),
             dma((2, 4, 4)),
             dma((2, 2, 2)),
-            dma((2,)),
+            dma((2, 3)),
             dma((2, 2, 4)),
             dma((3, NX)),
             dma((3, NX)),

time: 73 us -> 72.8 us (level)
  no operation moved by 1% of the time
where the time goes in v11:
time: 72.8 us; the launch traced here: 72.7 us
  Pallas kernels  71.1 us (98%)
  local copies, waits for them, and re-layouts  1.54 us (2%)
    pallas_call x1, Pallas kernels, body(): pl.pallas_call(kernel, out_shape=jax.ShapeDtypeStruct(tokens.shape, token...  71.1 us
    unnamed x1, local copies, waits for them, and re-layouts  1.54 us

profile of v11, /device:TPU:1, one launch (start us, length us, event | category | flops | bytes accessed | tf_op | source)
XLA Modules:
  0.0 72.7 jit_solution(4624346600646868330)
XLA Ops:
  0.0 71.1 %shard_map.46 = bf16[16,3072]{1,0:T(8,128)(2,1)} custom-call(bf16[16,3072]{1,0:T(8,128)(2,1)} %tokens.1, bf16[3,48,256]{2,1,0:T(8,128)(2,1)} %bitcast.1, bf16[32,384]{1,0:T(8,128)(2,1)} %out_weight.1, s32[2]{0:T(128)} %kind_hbm.1), custom_call_target="tpu_custom_call" | custom-call | tf_op jit(solution)/shard_map/pallas_call | solution.py:586
  71.1 1.5 %copy.6 = bf16[16,3072]{1,0:T(8,128)(2,1)} copy(bf16[16,3072]{1,0:T(8,128)(2,1)} %shard_map.46) | data formatting | bytes 196608

commit v12 on v11

--- a/solution.py
+++ b/solution.py
@@ -266,10 +266,6 @@
 
     here = wbuf.at[:, along, pair, odd]
     grid.begin(here, here, grid.device)
-    grid.begin(
-        cross, here, lambda first, second: (frame_at(second, 2 * first + other), band)
-    )
-    remote(cross, here, z_send.at[0], z_recv.at[0], (beside, band)).start()
     beside_z = y * NZ + z + 1 - 2 * lax.rem(z, 2)
     beside_y = (y + 1 - 2 * lax.rem(y, 2)) * NZ + z
     remote(
@@ -278,6 +274,10 @@
     remote(
         tokens, tbuf.at[lax.rem(y, 2), band], z_send.at[2], z_recv.at[1 + core], (beside_y, 2 * x + 1)
     ).start()
+    grid.begin(
+        cross, here, lambda first, second: (frame_at(second, 2 * first + other), band)
+    )
+    remote(cross, here, z_send.at[0], z_recv.at[0], (beside, band)).start()
     for copy in own[1:5]:
         copy.wait()
     token_along_x(0, tbuf.at[odd, band])

time: 72.8 us -> 72.7 us (level)
  no operation moved by 1% of the time
where the time goes in v12:
time: 72.7 us; the launch traced here: 72.6 us
  Pallas kernels  71 us (98%)
  local copies, waits for them, and re-layouts  1.54 us (2%)
    pallas_call x1, Pallas kernels, body(): pl.pallas_call(kernel, out_shape=jax.ShapeDtypeStruct(tokens.shape, token...  71 us
    unnamed x1, local copies, waits for them, and re-layouts  1.54 us

profile of v12, /device:TPU:1, one launch (start us, length us, event | category | flops | bytes accessed | tf_op | source)
XLA Modules:
  0.0 72.6 jit_solution(18342141476323137937)
XLA Ops:
  0.0 71.0 %shard_map.46 = bf16[16,3072]{1,0:T(8,128)(2,1)} custom-call(bf16[16,3072]{1,0:T(8,128)(2,1)} %tokens.1, bf16[3,48,256]{2,1,0:T(8,128)(2,1)} %bitcast.1, bf16[32,384]{1,0:T(8,128)(2,1)} %out_weight.1, s32[2]{0:T(128)} %kind_hbm.1), custom_call_target="tpu_custom_call" | custom-call | tf_op jit(solution)/shard_map/pallas_call | solution.py:586
  71.0 1.5 %copy.6 = bf16[16,3072]{1,0:T(8,128)(2,1)} copy(bf16[16,3072]{1,0:T(8,128)(2,1)} %shard_map.46) | data formatting | bytes 196608

commit v13 on v12

--- a/solution.py
+++ b/solution.py
@@ -295,7 +295,6 @@
             + lax.rem(row, SHARE)
         )
 
-    qkv_sum[...] = jnp.zeros_like(qkv_sum)
     by_peer[...] = jnp.where(wide == origin(tall), 1.0, 0.0).astype(jnp.bfloat16)
     by_frame[...] = jnp.where(tall == origin(wide), 1.0, 0.0).astype(jnp.bfloat16)
     bias[...] = jnp.where(lax.rem(tall, SHARE) == lax.rem(wide, SHARE), 0.0, -1e30)
@@ -380,13 +379,13 @@
         lax.fori_loop(0, PAIRS, one, 0)
 
     ring_step(1)
-    out_beyond()
     for hop in (1, NX - 1):
         await_bytes(tbuf.at[odd, band_at(-hop)], t_recv.at[0, hop])
     token_passed_on(0, sign)
     token_to_sibling(1)
     token_to_sibling(NX - 1)
     ring_step(2)
+    out_beyond()
     for which, by in ((1, 1), (2, -1)):
         for hop in (1, NX - 1):
             await_bytes(
@@ -410,40 +409,29 @@
         await_bytes(obuf.at[half, out_here(half)[1], 0 : NY - 3], o_recv1.at[half, 2])
     out_along_second(0)
 
-    chunk = 2 * NZ * DEPTH
-
-    def project(step, right):
-        at = pl.ds(pl.multiple_of(step * chunk, HEAD), chunk)
-        qkv_sum[...] += jnp.dot(
-            tbuf[:, :, :, at].reshape(ROWS, chunk),
+    def project(right):
+        qkv_sum[...] = jnp.dot(
+            tbuf[...].reshape(ROWS, -1),
             jnp.concatenate([right(slot) for slot in range(3)], axis=1),
             preferred_element_type=jnp.float32,
         )
 
     @pl.when(core == 0)
     def _():
-        def one(step, carry):
-            project(step, lambda slot: wbuf[slot, pl.ds(2 * step, 2)].reshape(chunk, HEAD))
-            return carry
-
-        lax.fori_loop(0, NY // 2, one, 0)
+        project(lambda slot: wbuf[slot].reshape(-1, HEAD))
 
     @pl.when(core == 1)
     def _():
-        def one(step, carry):
-            project(
-                step,
-                lambda slot: jnp.concatenate(
-                    [
-                        wbuf[slot, :, step, parity].reshape(chunk // 2, HEAD)
-                        for parity in range(2)
-                    ],
-                    axis=0,
-                ),
+        project(
+            lambda slot: jnp.concatenate(
+                [
+                    wbuf[slot, :, there, parity].reshape(-1, HEAD)
+                    for there in range(PAIRS)
+                    for parity in range(2)
+                ],
+                axis=0,
             )
-            return carry
-
-        lax.fori_loop(0, NY // 2, one, 0)
+        )
 
     rounded = qkv_sum[...].astype(jnp.bfloat16)
 

time: 72.7 us -> 72.8 us (level)
  no operation moved by 1% of the time
where the time goes in v13:
time: 72.8 us; the launch traced here: 72.7 us
  Pallas kernels  71.1 us (98%)
  local copies, waits for them, and re-layouts  1.54 us (2%)
    pallas_call x1, Pallas kernels, body(): pl.pallas_call(kernel, out_shape=jax.ShapeDtypeStruct(tokens.shape, token...  71.1 us
    unnamed x1, local copies, waits for them, and re-layouts  1.54 us

profile of v13, /device:TPU:1, one launch (start us, length us, event | category | flops | bytes accessed | tf_op | source)
XLA Modules:
  0.0 72.7 jit_solution(7701138666234708448)
XLA Ops:
  0.0 71.1 %shard_map.46 = bf16[16,3072]{1,0:T(8,128)(2,1)} custom-call(bf16[16,3072]{1,0:T(8,128)(2,1)} %tokens.1, bf16[3,48,256]{2,1,0:T(8,128)(2,1)} %bitcast.1, bf16[32,384]{1,0:T(8,128)(2,1)} %out_weight.1, s32[2]{0:T(128)} %kind_hbm.1), custom_call_target="tpu_custom_call" | custom-call | tf_op jit(solution)/shard_map/pallas_call | solution.py:574
  71.2 1.5 %copy.6 = bf16[16,3072]{1,0:T(8,128)(2,1)} copy(bf16[16,3072]{1,0:T(8,128)(2,1)} %shard_map.46) | data formatting | bytes 196608

commit v14 on v12

--- a/solution.py
+++ b/solution.py
@@ -110,8 +110,10 @@
         await_bytes(block, self.recv1.at[place])
         for way in range(2):
             self.to_second(block, way, 0, place)
-
-    def along_second(self, step, place):
+            if place == self.n_first - 1:
+                self.to_second(block, way, 1, place, 2)
+
+    def along_second(self, step, place, pass_on=True):
         for way in range(2):
             if step > hops(self.n_second)[way]:
                 continue
@@ -120,7 +122,7 @@
                 wrap(self.second - self.turn(way, place) * step, self.n_second),
             )
             await_bytes(block, self.recv2.at[way, step - 1, place])
-            if step < 3:
+            if step < 3 and pass_on:
                 self.to_second(block, way, step, place)
             if step == 2 and way == 0:
                 self.to_second(block, way, 3, place, 2)
@@ -372,14 +374,15 @@
     for place in range(1, PAIRS):
         grid.along_first(place)
 
-    def ring_step(step):
+    def ring_step(step, count=PAIRS):
         def one(place, carry):
             grid.along_second(step, place)
             return carry
 
-        lax.fori_loop(0, PAIRS, one, 0)
-
-    ring_step(1)
+        lax.fori_loop(0, count, one, 0)
+
+    ring_step(1, PAIRS - 1)
+    grid.along_second(1, PAIRS - 1, False)
     out_beyond()
     for hop in (1, NX - 1):
         await_bytes(tbuf.at[odd, band_at(-hop)], t_recv.at[0, hop])

time: 72.7 us -> 74.1 us (1.019)
  Pallas kernels: 71 us -> 72.4 us
    pallas_call x1, Pallas kernels: 71 us -> 72.4 us  [body(): pl.pallas_call(kernel, out_shape=jax.ShapeDtypeStruct(tokens.shape, token...]
where the time goes in v14:
time: 74.1 us; the launch traced here: 74 us
  Pallas kernels  72.4 us (98%)
  local copies, waits for them, and re-layouts  1.54 us (2%)
    pallas_call x1, Pallas kernels, body(): pl.pallas_call(kernel, out_shape=jax.ShapeDtypeStruct(tokens.shape, token...  72.4 us
    unnamed x1, local copies, waits for them, and re-layouts  1.54 us

profile of v14, /device:TPU:1, one launch (start us, length us, event | category | flops | bytes accessed | tf_op | source)
XLA Modules:
  0.0 74.0 jit_solution(11931949206539484007)
XLA Ops:
  0.0 72.4 %shard_map.46 = bf16[16,3072]{1,0:T(8,128)(2,1)} custom-call(bf16[16,3072]{1,0:T(8,128)(2,1)} %tokens.1, bf16[3,48,256]{2,1,0:T(8,128)(2,1)} %bitcast.1, bf16[32,384]{1,0:T(8,128)(2,1)} %out_weight.1, s32[2]{0:T(128)} %kind_hbm.1), custom_call_target="tpu_custom_call" | custom-call | tf_op jit(solution)/shard_map/pallas_call | solution.py:589
  72.4 1.5 %copy.6 = bf16[16,3072]{1,0:T(8,128)(2,1)} copy(bf16[16,3072]{1,0:T(8,128)(2,1)} %shard_map.46) | data formatting | bytes 196608

commit v15 on v12

--- a/solution.py
+++ b/solution.py
@@ -73,8 +73,8 @@
         flip = 1 - 2 * (place // 2 if isinstance(place, int) else lax.div(place, 2))
         return (self.sign if way == 0 else -self.sign) * flip
 
-    def to_second(self, block, way, step, place, by=1):
-        there = wrap(self.second + by * self.turn(way, place), self.n_second)
+    def to_second(self, block, way, step, place):
+        there = wrap(self.second + self.turn(way, place), self.n_second)
         remote(
             block,
             block,
@@ -120,10 +120,8 @@
                 wrap(self.second - self.turn(way, place) * step, self.n_second),
             )
             await_bytes(block, self.recv2.at[way, step - 1, place])
-            if step < 3:
+            if step < hops(self.n_second)[way]:
                 self.to_second(block, way, step, place)
-            if step == 2 and way == 0:
-                self.to_second(block, way, 3, place, 2)
 
 
 def kernel(

time: 72.7 us -> 73.3 us (level)
  no operation moved by 1% of the time
where the time goes in v15:
time: 73.3 us; the launch traced here: 73.2 us
  Pallas kernels  71.6 us (98%)
  local copies, waits for them, and re-layouts  1.54 us (2%)
    pallas_call x1, Pallas kernels, body(): pl.pallas_call(kernel, out_shape=jax.ShapeDtypeStruct(tokens.shape, token...  71.6 us
    unnamed x1, local copies, waits for them, and re-layouts  1.54 us

profile of v15, /device:TPU:1, one launch (start us, length us, event | category | flops | bytes accessed | tf_op | source)
XLA Modules:
  0.0 73.2 jit_solution(16447515029036226533)
XLA Ops:
  0.0 71.6 %shard_map.46 = bf16[16,3072]{1,0:T(8,128)(2,1)} custom-call(bf16[16,3072]{1,0:T(8,128)(2,1)} %tokens.1, bf16[3,48,256]{2,1,0:T(8,128)(2,1)} %bitcast.1, bf16[32,384]{1,0:T(8,128)(2,1)} %out_weight.1, s32[2]{0:T(128)} %kind_hbm.1), custom_call_target="tpu_custom_call" | custom-call | tf_op jit(solution)/shard_map/pallas_call | solution.py:584
  71.6 1.5 %copy.6 = bf16[16,3072]{1,0:T(8,128)(2,1)} copy(bf16[16,3072]{1,0:T(8,128)(2,1)} %shard_map.46) | data formatting | bytes 196608

commit v16 on v12

--- a/solution.py
+++ b/solution.py
@@ -381,12 +381,12 @@
 
     ring_step(1)
     out_beyond()
+    ring_step(2)
     for hop in (1, NX - 1):
         await_bytes(tbuf.at[odd, band_at(-hop)], t_recv.at[0, hop])
     token_passed_on(0, sign)
     token_to_sibling(1)
     token_to_sibling(NX - 1)
-    ring_step(2)
     for which, by in ((1, 1), (2, -1)):
         for hop in (1, NX - 1):
             await_bytes(

time: 72.7 us -> 73 us (level)
  no operation moved by 1% of the time
where the time goes in v16:
time: 73 us; the launch traced here: 72.8 us
  Pallas kernels  71.3 us (98%)
  local copies, waits for them, and re-layouts  1.54 us (2%)
    pallas_call x1, Pallas kernels, body(): pl.pallas_call(kernel, out_shape=jax.ShapeDtypeStruct(tokens.shape, token...  71.3 us
    unnamed x1, local copies, waits for them, and re-layouts  1.54 us

profile of v16, /device:TPU:1, one launch (start us, length us, event | category | flops | bytes accessed | tf_op | source)
XLA Modules:
  0.0 72.8 jit_solution(14672276697237102966)
XLA Ops:
  0.0 71.3 %shard_map.46 = bf16[16,3072]{1,0:T(8,128)(2,1)} custom-call(bf16[16,3072]{1,0:T(8,128)(2,1)} %tokens.1, bf16[3,48,256]{2,1,0:T(8,128)(2,1)} %bitcast.1, bf16[32,384]{1,0:T(8,128)(2,1)} %out_weight.1, s32[2]{0:T(128)} %kind_hbm.1), custom_call_target="tpu_custom_call" | custom-call | tf_op jit(solution)/shard_map/pallas_call | solution.py:586
  71.3 1.5 %copy.6 = bf16[16,3072]{1,0:T(8,128)(2,1)} copy(bf16[16,3072]{1,0:T(8,128)(2,1)} %shard_map.46) | data formatting | bytes 196608

commit v17 on v12

--- a/solution.py
+++ b/solution.py
@@ -406,9 +406,6 @@
                 )
     ring_step(4)
     await_bytes(wbuf.at[:, along, pair, other], z_recv.at[0])
-    for half in range(2):
-        await_bytes(obuf.at[half, out_here(half)[1], 0 : NY - 3], o_recv1.at[half, 2])
-    out_along_second(0)
 
     chunk = 2 * NZ * DEPTH
 
@@ -445,6 +442,9 @@
 
         lax.fori_loop(0, NY // 2, one, 0)
 
+    for half in range(2):
+        await_bytes(obuf.at[half, out_here(half)[1], 0 : NY - 3], o_recv1.at[half, 2])
+    out_along_second(0)
     rounded = qkv_sum[...].astype(jnp.bfloat16)
 
     msg[...] = (
@@ -555,7 +555,7 @@
     def columns(which):
         return out.at[:, pl.ds(pl.multiple_of(which * WIDTH, HEAD), WIDTH)]
 
-    for step in range(1, BANDS):
+    for step in (4, 5, 3, 6, 2, 7, 1):
         there = wrap(band + step, BANDS)
         remote(
             sbuf.at[there], columns(band), f_send.at[step], f_recv.at[step], (frame, there)

time: 72.7 us -> 73.6 us (1.012)
  Pallas kernels: 71 us -> 71.9 us
    pallas_call x1, Pallas kernels: 71 us -> 71.9 us  [body(): pl.pallas_call(kernel, out_shape=jax.ShapeDtypeStruct(tokens.shape, token...]
where the time goes in v17:
time: 73.6 us; the launch traced here: 73.5 us
  Pallas kernels  71.9 us (98%)
  local copies, waits for them, and re-layouts  1.54 us (2%)
    pallas_call x1, Pallas kernels, body(): pl.pallas_call(kernel, out_shape=jax.ShapeDtypeStruct(tokens.shape, token...  71.9 us
    unnamed x1, local copies, waits for them, and re-layouts  1.54 us

profile of v17, /device:TPU:1, one launch (start us, length us, event | category | flops | bytes accessed | tf_op | source)
XLA Modules:
  0.0 73.5 jit_solution(14427011411509015258)
XLA Ops:
  0.0 71.9 %shard_map.46 = bf16[16,3072]{1,0:T(8,128)(2,1)} custom-call(bf16[16,3072]{1,0:T(8,128)(2,1)} %tokens.1, bf16[3,48,256]{2,1,0:T(8,128)(2,1)} %bitcast.1, bf16[32,384]{1,0:T(8,128)(2,1)} %out_weight.1, s32[2]{0:T(128)} %kind_hbm.1), custom_call_target="tpu_custom_call" | custom-call | tf_op jit(solution)/shard_map/pallas_call | solution.py:586
  71.9 1.5 %copy.6 = bf16[16,3072]{1,0:T(8,128)(2,1)} copy(bf16[16,3072]{1,0:T(8,128)(2,1)} %shard_map.46) | data formatting | bytes 196608
